TPU v7x, 32 devices: a whole 2x2x4 slice. The times are simulated.
32 devices in a mesh: groups: 2 (over x), dp: 16 (over z, y, core).
Axes of the slice: x: 2, y: 2, z: 4, core: 2. Of those that a mesh axis runs over, the one named last changes fastest.
Arguments:
- tokens: bfloat16 [4096, 8192], P(('groups', 'dp')), parts along dimension 0, may hold values from -6 to 6
- out_grad: bfloat16 [4096, 512], P(('groups', 'dp')), parts along dimension 0, may hold values from -6 to 6
- base_weight: bfloat16 [8192, 512], P('dp'), may hold values from -0.0625 to 0.0625
- adapter_down: bfloat16 [16, 64, 8192], P(None, None, 'dp'), may hold values from -0.0625 to 0.0625
- adapter_up: bfloat16 [16, 32768], P(None, 'dp'), may hold values from -0.75 to 0.75
- rank_tiles: int32 [16], replicated, may hold values from 1 to 4, as said below
- tile_adapter: int32 [32, 1], P('groups'), parts along dimension 0, may hold values from 0 to 15
Outputs:
- result: bfloat16 [4096, 512], P(('groups', 'dp')), parts along dimension 0
- grad_in: bfloat16 [4096, 8192], P(('groups', 'dp')), parts along dimension 0
- down_grad: bfloat16 [32, 64, 8192], P('groups', None, 'dp'), parts along dimension 0
- up_grad: bfloat16 [32, 32768], P('groups', 'dp'), parts along dimension 0
There are 2 independent parts, one for each index of `groups`. A program takes and returns all parts, laid end to end along the dimension named above; an argument that names none is the same for every part. Nothing has to cross between parts.
Inputs may be any that keep to these rules, and one draw needn't show every extreme that they name: `rank_tiles`: ranks of 1 and of 4 tiles occur in every draw. `tile_adapter`: every adapter is used by at least one tile.
All inputs are finite; a program needn't handle non-finite values.
Results may differ from a plain program's by a relative error of at most 0.005.
Values may be sent and summed in bfloat16 or wider, within the bound.
No kernel may reach another device: no remote copies, remote signals or barrier semaphores. Data moves between devices by JAX's collectives and lax.ppermute only.
A program may use at most 64 MiB of HBM per device.

v0:
```python
import functools

import jax
import jax.numpy as jnp
from jax import lax
from jax.experimental import pallas as pl
from jax.experimental.pallas import tpu as pltpu
from jax.sharding import PartitionSpec as P

RANK_TILE = 16
AXES = ("groups", "dp")
F32 = jnp.float32
BF16 = jnp.bfloat16
VMEM = pl.BlockSpec(memory_space=pltpu.VMEM)
SMEM = pl.BlockSpec(memory_space=pltpu.SMEM)


def dot(a, b, ca, cb):
    return lax.dot_general(a, b, (((ca,), (cb,)), ((), ())), preferred_element_type=F32)


def call(kernel, outs, scalars, arrays, flops=0):
    size = sum(x.size * x.dtype.itemsize for x in arrays)
    size += sum(x.size * x.dtype.itemsize for x in outs)
    return pl.pallas_call(
        kernel,
        out_shape=outs,
        in_specs=[SMEM] * len(scalars) + [VMEM] * len(arrays),
        out_specs=[VMEM] * len(outs),
        compiler_params=pltpu.CompilerParams(vmem_limit_bytes=30 * 1024 * 1024),
        cost_estimate=pl.CostEstimate(flops=flops, bytes_accessed=size, transcendentals=0),
    )(*scalars, *arrays)


def shape(dims, dtype=BF16):
    return jax.ShapeDtypeStruct(dims, dtype)


def iota(dims, axis):
    return lax.broadcasted_iota(jnp.int32, dims, axis)


def factor_of(ids, ranks, tile, width):
    count = ranks[ids[tile]]
    scale = 2.0 / jnp.full((1, width), count, jnp.int32).astype(F32)
    return jnp.where(iota((1, width), 1) < count * RANK_TILE, scale, 0.0)


def pack_kernel(meta, ids, down, up_own, up_other, blocks):
    adapters, rank, width = down.shape
    chips = blocks.shape[0]
    c = meta[1]
    rows = chips * 16
    q = iota((rows, adapters), 0)
    chosen = jnp.zeros((rows, adapters), jnp.int32)
    for chip in range(chips):
        for slot in range(2):
            adapter = ids[2 * chip + jnp.bitwise_xor(c, slot)]
            blocks[chip, rank * slot : rank * (slot + 1), :] = down[adapter]
            chosen = jnp.where(q // 8 == 2 * chip + slot, adapter, chosen)
    match = chosen == iota((rows, adapters), 1)
    packed = jnp.zeros((rows, width), F32)
    for side, up in enumerate((up_own, up_other)):
        for r in range(4):
            pick = (match & (q % 8 == 4 * side + r)).astype(F32).astype(BF16)
            packed = packed + dot(pick, up[:, width * r : width * (r + 1)], 1, 0)
    packed = packed.astype(BF16)
    for chip in range(chips):
        blocks[chip, 2 * rank : 2 * rank + 16, :] = packed[16 * chip : 16 * (chip + 1), :]


def lane_masks(out_width, width, rank):
    per_row = width // rank
    lane_ok = iota((out_width, width), 1) // rank == iota((out_width, width), 0) % per_row
    fold = (iota((width, rank), 0) % rank == iota((width, rank), 1)).astype(F32).astype(BF16)
    return lane_ok, fold


def rank_kernel(
    meta, ids, ranks, tok_own, tok_sib, og_own, og_sib, blocks, grads, low, back_own, back_sib, up_out
):
    chips, _, width = blocks.shape
    rows = tok_own.shape[0]
    out_width = og_own.shape[1]
    rank = back_own.shape[1]
    k, c = meta[0], meta[1]
    heads = out_width // (2 * chips)
    per_row = width // rank
    packed = jnp.concatenate([blocks[i, 2 * rank : 2 * rank + 16, :] for i in range(chips)], axis=0)
    q = iota((out_width, chips * 16), 1)
    o = iota((out_width, chips * 16), 0)
    device = 2 * (q // 16) + jnp.bitwise_xor(c, (q // 4) % 2)
    place = o // per_row == device * (heads // per_row) + q % 4
    lane_ok, fold = lane_masks(out_width, width, rank)
    for slot, (tok, og, back) in enumerate(
        ((tok_own, og_own, back_own), (tok_sib, og_sib, back_sib))
    ):
        pick = (place & ((q // 8) % 2 == slot)).astype(F32).astype(BF16)
        spread = jnp.where(lane_ok, dot(pick, packed, 1, 0), 0.0).astype(BF16)
        up = dot(spread, fold, 1, 0).astype(BF16)
        if slot == 0:
            up_out[...] = up
        factor = factor_of(ids, ranks, 2 * k + jnp.bitwise_xor(c, slot), rank)
        backward = (dot(og[...], up, 1, 0) * factor).astype(BF16)
        back[...] = backward
        turned = backward.T
        total = jnp.zeros((rows, rank), F32)
        half = slice(rank * slot, rank * (slot + 1))
        for i in range(chips):
            start = pl.multiple_of((2 * i + c) * width, width)
            part = tok[:, pl.ds(start, width)]
            grads[i, half, :] = dot(turned, part, 1, 0).astype(BF16)
            total = total + dot(part, blocks[i, half, :], 1, 1)
        low[rows * slot : rows * (slot + 1), :] = total


def hidden_kernel(meta, ids, ranks, low, other, og_own, og_sib, up, grads, out_low, terms):
    chips, _, width = terms.shape
    rows, out_width = og_own.shape
    rank = up.shape[1]
    k, c = meta[0], meta[1]
    heads = out_width // (2 * chips)
    per_row = width // rank
    q = iota((chips * 16, out_width), 0)
    o = iota((chips * 16, out_width), 1)
    place = o // per_row == (2 * (q // 16) + c) * (heads // per_row) + q % 4
    lane_ok, fold = lane_masks(out_width, width, rank)
    packed = jnp.zeros((chips * 16, width), F32)
    for slot, og in enumerate((og_own, og_sib)):
        factor = factor_of(ids, ranks, 2 * k + jnp.bitwise_xor(c, slot), rank)
        total = low[rows * slot : rows * (slot + 1), :] + other[rows * (1 - slot) : rows * (2 - slot), :]
        hidden = (total * factor).astype(BF16)
        if slot == 0:
            out_low[...] = dot(hidden, up[...], 1, 1)
        term = dot(og[...], hidden, 0, 0).astype(BF16)
        spread = jnp.where(lane_ok, dot(term, fold, 1, 1), 0.0).astype(BF16)
        pick = (place & ((q // 4) % 4 == slot)).astype(F32).astype(BF16)
        packed = packed + dot(pick, spread, 1, 0)
    terms[...] = packed.astype(BF16).reshape(terms.shape)


def base_kernel(plan, meta, tok_own, tok_sib, og_own, og_sib, back_own, back_sib, blocks, *refs):
    pieces = refs[: len(refs) - 4]
    for_own, for_sib, grad_own, grad_sib = refs[len(refs) - 4 :]
    width = blocks.shape[2]
    rank = back_own.shape[1]
    rows = tok_own.shape[0]
    k, c, g = meta[0], meta[1], meta[2]
    og = jnp.concatenate([og_own[...], og_sib[...]], axis=0)
    total = jnp.zeros((2 * rows, og.shape[1]), F32)
    for index, j, count, side in plan:
        piece = pieces[index]
        chip = jnp.bitwise_xor(k, j)
        shift = 0 if side is None else jnp.bitwise_xor(g, side) * count
        if piece.shape[0] > count:
            weight = piece[pl.ds(pl.multiple_of(chip * count, count), count), :]
        else:
            weight = piece[...]
        start = pl.multiple_of((2 * chip + c) * width + shift, 128)
        tok = jnp.concatenate(
            [tok_own[:, pl.ds(start, count)], tok_sib[:, pl.ds(start, count)]], axis=0
        )
        total = total + dot(tok, weight, 1, 0)
        grad = dot(og, weight, 1, 1)
        inner = pl.ds(pl.multiple_of(shift, 128), count)
        low_own = dot(back_own[...], blocks[chip, 0:rank, inner], 1, 0).astype(BF16)
        low_sib = dot(back_sib[...], blocks[chip, rank : 2 * rank, inner], 1, 0).astype(BF16)
        to = pl.ds(pl.multiple_of(chip * width + shift, 128), count)
        grad_own[:, to] = (grad[:rows] + low_own.astype(F32)).astype(BF16)
        grad_sib[:, to] = (grad[rows:] + low_sib.astype(F32)).astype(BF16)
    for_own[...] = total[:rows]
    for_sib[...] = total[rows:]


def join_kernel(chips, meta, mine, other, out_low, grad_mine, grad_other, result, grad_in):
    c = meta[1]
    result[...] = (mine[...] + other[...] + out_low[...]).astype(BF16)
    width = grad_mine.shape[1] // chips
    for chip in range(chips):
        cols = slice(width * chip, width * (chip + 1))
        own = pl.multiple_of((2 * chip + c) * width, width)
        sib = pl.multiple_of((2 * chip + 1 - c) * width, width)
        grad_in[:, pl.ds(own, width)] = grad_mine[:, cols]
        grad_in[:, pl.ds(sib, width)] = grad_other[:, cols]


def back_kernel(meta, ids, back, down_out, up_out):
    rank = down_out.shape[1]
    chips, _, width = back.shape
    c = meta[1]
    flat = jnp.concatenate([back[i, 2 * rank : 2 * rank + 16, :] for i in range(chips)], axis=0)
    q = iota((up_out.shape[0], chips * 16), 1)
    chosen = jnp.full(q.shape, -1, jnp.int32)
    for chip in range(chips):
        for slot in range(2):
            adapter = ids[2 * chip + jnp.bitwise_xor(c, slot)]
            down_out[adapter] = back[chip, rank * slot : rank * (slot + 1), :]
            chosen = jnp.where(q // 4 == 4 * chip + slot, adapter, chosen)
    match = chosen == iota(q.shape, 0)
    for r in range(4):
        pick = (match & (q % 4 == r)).astype(F32).astype(BF16)
        up_out[:, width * r : width * (r + 1)] = dot(pick, flat, 1, 0).astype(BF16)


def after(x, *others):
    return lax.optimization_barrier((x, *others))[0]


def pairs(groups, size, to):
    out = []
    for g in range(groups):
        for d in range(size):
            target = to(g, d)
            if target is not None:
                out.append((g * size + d, target[0] * size + target[1]))
    return out


def gather_weight(weight, groups, size, send, packed):
    chips = size // 2
    rows = weight.shape[0]
    if groups != 2 or chips != 8:
        lists = [[2 * chip + core for chip in range(chips)] for core in range(2)]
        full = lax.all_gather(weight, "dp", axis=0, tiled=True, axis_index_groups=lists)
        return [full], [(0, j, rows, None) for j in range(chips)], (), ()
    half = rows // 2
    mine = lax.dynamic_slice_in_dim(weight, lax.axis_index("groups") * half, half)
    swap_x = lambda g, d: (1 - g, d)
    swap_y = lambda g, d: (g, d ^ 2)
    far = send(mine, lambda g, d: (g, d ^ 12))
    near = send(mine, lambda g, d: (g, d ^ 4))
    own_y = send(weight, swap_y)
    far_near = send(after(far, packed), lambda g, d: (g, d ^ 4))
    arrays = [weight, own_y]
    plan = [(0, 0, rows, None), (1, 1, rows, None)]
    for j, held in ((2, near), (6, far), (4, far_near)):
        over_y = send(held, swap_y)
        first = len(arrays)
        arrays += [held, send(held, swap_x), over_y, send(over_y, swap_x)]
        plan += [(first + i, j + i // 2, half, i % 2) for i in range(4)]
    return arrays, plan, (own_y, near, far), arrays[:-1]


def body(groups, size, tokens, out_grad, base_weight, adapter_down, adapter_up, rank_tiles, tile_adapter):
    chips = size // 2
    rows, model_width = tokens.shape
    out_width = out_grad.shape[1]
    adapters, rank, width = adapter_down.shape
    ids = tile_adapter[:, 0]
    place = lax.axis_index("dp")
    meta = jnp.stack([place // 2, place % 2, lax.axis_index("groups")]).astype(jnp.int32)

    def send(x, to):
        return lax.ppermute(x, AXES, pairs(groups, size, to))

    def sibling(x):
        return send(x, lambda g, d: (g, d ^ 1))

    same_core = [[2 * chip + core for chip in range(chips)] for core in range(2)]

    def exchange(blocks):
        return lax.all_to_all(
            blocks, "dp", split_axis=0, concat_axis=0, tiled=True, axis_index_groups=same_core
        )

    up_sib = sibling(adapter_up)
    tok_sib = sibling(tokens)
    og_sib = sibling(out_grad)
    (packed,) = call(
        pack_kernel,
        [shape((chips, 2 * rank + 16, width))],
        (meta, ids),
        (adapter_down, adapter_up, up_sib),
    )
    weights, plan, first, early = gather_weight(base_weight, groups, size, send, packed)
    blocks = exchange(after(packed, tok_sib, og_sib, *first))

    grads, low, back_own, back_sib, up_mine = call(
        rank_kernel,
        [
            shape((chips, 2 * rank + 16, width)),
            shape((2 * rows, rank), F32),
            shape((rows, rank)),
            shape((rows, rank)),
            shape((out_width, rank)),
        ],
        (meta, ids, rank_tiles),
        (tokens, tok_sib, out_grad, og_sib, blocks),
        flops=4 * rows * model_width * rank,
    )
    size_up = pl.BlockSpec((chips, 16, width), lambda i: (0, rank // 8, 0))
    out_low, grads = pl.pallas_call(
        hidden_kernel,
        grid=(1,),
        out_shape=[shape((rows, out_width), F32), shape(grads.shape)],
        in_specs=[SMEM] * 3 + [VMEM] * 5 + [pl.BlockSpec(memory_space=pl.ANY)],
        out_specs=[pl.BlockSpec((rows, out_width), lambda i: (0, 0)), size_up],
        input_output_aliases={8: 1},
        compiler_params=pltpu.CompilerParams(vmem_limit_bytes=30 * 1024 * 1024),
    )(meta, ids, rank_tiles, low, sibling(low), after(out_grad, *early), og_sib, up_mine, grads)
    grads_back = exchange(grads)

    for_own, for_sib, grad_own, grad_sib = call(
        functools.partial(base_kernel, plan),
        [shape((rows, out_width), F32)] * 2 + [shape((rows, model_width // 2))] * 2,
        (meta,),
        (tokens, tok_sib, out_grad, og_sib, after(back_own, out_low), back_sib, blocks, *weights),
        flops=4 * rows * model_width * out_width,
    )
    for_other, grad_other = sibling(for_sib), sibling(grad_sib)
    result, grad_in = call(
        functools.partial(join_kernel, chips),
        [shape((rows, out_width)), shape((rows, model_width))],
        (meta,),
        (for_own, for_other, out_low, grad_own, grad_other),
    )
    down_grad, up_grad = call(
        back_kernel,
        [shape(adapter_down.shape), shape(adapter_up.shape)],
        (meta, ids),
        (grads_back,),
    )
    return result, grad_in, down_grad, up_grad


def solution(mesh):
    return jax.shard_map(
        functools.partial(body, mesh.shape["groups"], mesh.shape["dp"]),
        mesh=mesh,
        in_specs=(
            P(("groups", "dp"), None),
            P(("groups", "dp"), None),
            P("dp", None),
            P(None, None, "dp"),
            P(None, "dp"),
            P(),
            P("groups", None),
        ),
        out_specs=(
            P(("groups", "dp"), None),
            P(("groups", "dp"), None),
            P("groups", None, "dp"),
            P("groups", "dp"),
        ),
        check_vma=False,
    )
```

profile of v0, /device:TPU:0, one launch (start us, length us, event | category | flops | bytes accessed | tf_op | source)
XLA Modules:
  0.0 104.3 jit_solution(9007735857167601354)
XLA Ops:
  0.6 0.5 collective-permute-start
  1.1 2.6 %collective-permute-start.3 = (bf16[512,512]{1,0:T(8,128)(2,1)}, bf16[512,512]{1,0:T(8,128)(2,1)S(1)}, u32[]{:S(2)}, u32[]{:S(2)}) collective-permute-start(bf16[512,512]{1,0:T(8,128)(2,1)} %refs_0_.1), channel_id=1, source_target_pairs={{0,2},{1,3},{2,0},{3,1},{4,6},{5,7},{6,4},{7,5},{8,10},{9,11},{10,... | collective-permute-start | bytes 1572872 | tf_op jit(solution)/shard_map/ppermute | solution.py:254
  3.7 1.0 constant_dynamic-slice_fusion
  4.7 3.7 %collective-permute-start.5 = (bf16[256,512]{1,0:T(8,128)(2,1)S(1)}, bf16[256,512]{1,0:T(8,128)(2,1)}, u32[]{:S(2)}, u32[]{:S(2)}) collective-permute-start(bf16[256,512]{1,0:T(8,128)(2,1)S(1)} %constant_dynamic-slice_fusion), channel_id=1, source_target_pairs={{0,12},{1,13},{2,14},{3,15},{4,8},{5,9},{6,10},{7,11},{8,4},{9,5},... | collective-permute-start | bytes 786440 | tf_op jit(solution)/shard_map/ppermute | solution.py:254
  8.4 0.0 collective-permute-start.4
  8.4 0.0 collective-permute-start.2
  8.4 1.5 %collective-permute-done.2.up_other = bf16[16,2048]{1,0:T(8,128)(2,1)S(1)} collective-permute-done((bf16[16,2048]{1,0:T(8,128)(2,1)}, bf16[16,2048]{1,0:T(8,128)(2,1)S(1)}, u32[]{:S(2)}, u32[]{:S(2)}) %collective-permute-start.2) | collective-permute-done | bytes 65568 | tf_op jit(solution)/shard_map/ppermute | solution.py:254
  9.9 0.2 collective-permute-start.1
  10.0 0.1 pad_add_fusion.meta
  10.1 1.2 %copy-done.5 = bf16[16,64,512]{2,1,0:T(8,128)(2,1)S(1)} copy-done((bf16[16,64,512]{2,1,0:T(8,128)(2,1)S(1)}, bf16[16,64,512]{2,1,0:T(8,128)(2,1)}, u32[]{:S(2)}) %copy-start.5) | copy-done | bytes 1048600
  11.3 0.8 copy-done.12
  12.2 0.7 copy-done.17
  12.8 1.0 shard_map.102
  13.8 0.0 copy-start.1
  13.8 1.0 copy-done.1
  14.9 0.0 collective-permute-done.1.og_sib
  14.9 1.1 %collective-permute-done.5.refs_6_ = bf16[256,512]{1,0:T(8,128)(2,1)} collective-permute-done((bf16[256,512]{1,0:T(8,128)(2,1)S(1)}, bf16[256,512]{1,0:T(8,128)(2,1)}, u32[]{:S(2)}, u32[]{:S(2)}) %collective-permute-start.5) | collective-permute-done | bytes 262176 | tf_op jit(solution)/shard_map/ppermute | solution.py:254
  15.9 4.9 %collective-permute-done.4.refs_2_ = bf16[256,512]{1,0:T(8,128)(2,1)} collective-permute-done((bf16[256,512]{1,0:T(8,128)(2,1)S(1)}, bf16[256,512]{1,0:T(8,128)(2,1)}, u32[]{:S(2)}, u32[]{:S(2)}) %collective-permute-start.4) | collective-permute-done | bytes 262176 | tf_op jit(solution)/shard_map/ppermute | solution.py:254
  20.9 0.0 collective-permute-done.3.refs_1_
  20.9 0.8 copy-done.6
  21.7 0.0 collective-permute-done.tok_sib
  21.7 3.6 %all-to-all-start = ((bf16[8,144,512]{2,1,0:T(8,128)(2,1)}), bf16[8,144,512]{2,1,0:T(8,128)(2,1)S(1)}, u32[]{:S(2)}, u32[]{:S(2)}) async-start(bf16[8,144,512]{2,1,0:T(8,128)(2,1)} %copy-done.1), calls=%async_computation | async-start | bytes 2359296 | tf_op jit(solution)/shard_map/all_to_all | solution.py:262
  25.2 1.9 %collective-permute-start.11 = (bf16[256,512]{1,0:T(8,128)(2,1)}, bf16[256,512]{1,0:T(8,128)(2,1)}, u32[]{:S(2)}, u32[]{:S(2)}) collective-permute-start(bf16[256,512]{1,0:T(8,128)(2,1)} %collective-permute-done.5.refs_6_), channel_id=1, source_target_pairs={{0,2},{1,3},{2,0},{3,1},{4,6},{5,7},{6,4},{7,5},{8,10},{9,11},{10,... | collective-permute-start | bytes 786440 | tf_op jit(solution)/shard_map/ppermute | solution.py:254
  27.2 0.2 collective-permute-start.8
  27.3 1.9 %collective-permute-start.13 = (bf16[256,512]{1,0:T(8,128)(2,1)}, bf16[256,512]{1,0:T(8,128)(2,1)}, u32[]{:S(2)}, u32[]{:S(2)}) collective-permute-start(bf16[256,512]{1,0:T(8,128)(2,1)} %collective-permute-done.5.refs_6_), channel_id=1, source_target_pairs={{0,4},{1,5},{2,6},{3,7},{4,0},{5,1},{6,2},{7,3},{8,12},{9,13},{10,... | collective-permute-start | bytes 786440 | tf_op jit(solution)/shard_map/ppermute | solution.py:254
  29.2 1.5 %collective-permute-start.10 = (bf16[256,512]{1,0:T(8,128)(2,1)}, bf16[256,512]{1,0:T(8,128)(2,1)S(1)}, u32[]{:S(2)}, u32[]{:S(2)}) collective-permute-start(bf16[256,512]{1,0:T(8,128)(2,1)} %collective-permute-done.5.refs_6_), channel_id=1, source_target_pairs={{0,16},{1,17},{2,18},{3,19},{4,20},{5,21},{6,22},{7,23},{8,24},{9,... | collective-permute-start | bytes 786440 | tf_op jit(solution)/shard_map/ppermute | solution.py:254
  30.7 0.5 collective-permute-start.7
  31.2 15.5 %collective-permute-done.11.refs_8_ = bf16[256,512]{1,0:T(8,128)(2,1)} collective-permute-done((bf16[256,512]{1,0:T(8,128)(2,1)}, bf16[256,512]{1,0:T(8,128)(2,1)}, u32[]{:S(2)}, u32[]{:S(2)}) %collective-permute-start.11) | collective-permute-done | bytes 262176 | tf_op jit(solution)/shard_map/ppermute | solution.py:254
  46.7 1.5 %collective-permute-start.12 = (bf16[256,512]{1,0:T(8,128)(2,1)}, bf16[256,512]{1,0:T(8,128)(2,1)}, u32[]{:S(2)}, u32[]{:S(2)}) collective-permute-start(bf16[256,512]{1,0:T(8,128)(2,1)} %collective-permute-done.11.refs_8_), channel_id=1, source_target_pairs={{0,16},{1,17},{2,18},{3,19},{4,20},{5,21},{6,22},{7,23},{8,24},{9,... | collective-permute-start | bytes 786440 | tf_op jit(solution)/shard_map/ppermute | solution.py:254
  48.2 3.7 %collective-permute-done.8.refs_4_ = bf16[256,512]{1,0:T(8,128)(2,1)} collective-permute-done((bf16[256,512]{1,0:T(8,128)(2,1)}, bf16[256,512]{1,0:T(8,128)(2,1)}, u32[]{:S(2)}, u32[]{:S(2)}) %collective-permute-start.8) | collective-permute-done | bytes 262176 | tf_op jit(solution)/shard_map/ppermute | solution.py:254
  51.9 1.5 %collective-permute-start.9 = (bf16[256,512]{1,0:T(8,128)(2,1)}, bf16[256,512]{1,0:T(8,128)(2,1)}, u32[]{:S(2)}, u32[]{:S(2)}) collective-permute-start(bf16[256,512]{1,0:T(8,128)(2,1)} %collective-permute-done.8.refs_4_), channel_id=1, source_target_pairs={{0,16},{1,17},{2,18},{3,19},{4,20},{5,21},{6,22},{7,23},{8,24},{9,... | collective-permute-start | bytes 786440 | tf_op jit(solution)/shard_map/ppermute | solution.py:254
  53.4 0.0 collective-permute-done.13.refs_10_
  53.4 0.0 collective-permute-start.15
  53.4 0.0 collective-permute-done.10.refs_7_
  53.5 0.7 copy-done.8
  54.1 0.5 collective-permute-start.14
  54.7 0.0 all-to-all-done.blocks
  54.7 4.3 %shard_map.103 = (bf16[8,144,512]{2,1,0:T(8,128)(2,1)S(1)}, f32[256,64]{1,0:T(8,128)S(1)}, bf16[128,64]{1,0:T(8,128)(2,1)S(1)}, bf16[128,64]{1,0:T(8,128)(2,1)S(1)}, bf16[512,64]{1,0:T(8,128)(2,1)S(1)}) custom-call(s32[3]{0:T(128)S(1)} %pad_add_fusion.meta, s32[16]{0:T(128)S(1)} %bitcast.5, s32[16]{0:T(128)S(1)} %copy-done.19, ...), custom_call_target="tpu_custom_call" | custom-call | flops 268435456 | bytes 6979584 | tf_op jit(solution)/shard_map/pallas_call | solution.py:25
  59.0 0.0 copy-start.13
  59.0 0.6 copy-done.13
  59.6 0.6 copy-done.15
  60.2 0.0 collective-permute-start.6
  60.2 0.0 collective-permute-done.12.refs_9_
  60.2 1.3 %collective-permute-done.9.refs_5_ = bf16[256,512]{1,0:T(8,128)(2,1)} collective-permute-done((bf16[256,512]{1,0:T(8,128)(2,1)}, bf16[256,512]{1,0:T(8,128)(2,1)}, u32[]{:S(2)}, u32[]{:S(2)}) %collective-permute-start.9) | collective-permute-done | bytes 262176 | tf_op jit(solution)/shard_map/ppermute | solution.py:254
  61.5 3.8 %collective-permute-done.14.refs_11_ = bf16[256,512]{1,0:T(8,128)(2,1)} collective-permute-done((bf16[256,512]{1,0:T(8,128)(2,1)}, bf16[256,512]{1,0:T(8,128)(2,1)}, u32[]{:S(2)}, u32[]{:S(2)}) %collective-permute-start.14) | collective-permute-done | bytes 262176 | tf_op jit(solution)/shard_map/ppermute | solution.py:254
  65.3 1.6 %shard_map.104 = (f32[128,512]{1,0:T(8,128)S(1)}, bf16[8,144,512]{2,1,0:T(8,128)(2,1)S(1)}) custom-call(s32[3]{0:T(128)S(1)} %pad_add_fusion.meta, s32[16]{0:T(128)S(1)} %bitcast.6, s32[16]{0:T(128)S(1)} %copy-done.19, f32[256,64]{1,0:T(8,128)S(1)} %get-tuple-element.25.low, ...), custom_call_target="tpu_custom_call", output_to_operand_aliasing={{1}: (8, {})} | custom-call | tf_op jit(solution)/shard_map/pallas_call | solution.py:292
  66.9 1.0 copy-done.2
  67.9 0.7 copy-done.10
  68.6 5.2 %all-to-all-start.1 = ((bf16[8,144,512]{2,1,0:T(8,128)(2,1)}), bf16[8,144,512]{2,1,0:T(8,128)(2,1)}, u32[]{:S(2)}, u32[]{:S(2)}) async-start(bf16[8,144,512]{2,1,0:T(8,128)(2,1)} %copy-done.2), calls=%async_computation.1 | async-start | bytes 2359296 | tf_op jit(solution)/shard_map/all_to_all | solution.py:262
  73.7 1.5 %collective-permute-start.16 = (bf16[256,512]{1,0:T(8,128)(2,1)}, bf16[256,512]{1,0:T(8,128)(2,1)S(1)}, u32[]{:S(2)}, u32[]{:S(2)}) collective-permute-start(bf16[256,512]{1,0:T(8,128)(2,1)} %collective-permute-done.15.refs_12_), channel_id=1, source_target_pairs={{0,16},{1,17},{2,18},{3,19},{4,20},{5,21},{6,22},{7,23},{8,24},{9,... | collective-permute-start | bytes 786440 | tf_op jit(solution)/shard_map/ppermute | solution.py:254
  75.2 5.8 %collective-permute-done.16.refs_13_ = bf16[256,512]{1,0:T(8,128)(2,1)S(1)} collective-permute-done((bf16[256,512]{1,0:T(8,128)(2,1)}, bf16[256,512]{1,0:T(8,128)(2,1)S(1)}, u32[]{:S(2)}, u32[]{:S(2)}) %collective-permute-start.16) | collective-permute-done | bytes 262176 | tf_op jit(solution)/shard_map/ppermute | solution.py:254
  81.1 1.0 copy-done.4
  82.1 1.0 copy-done.7
  83.1 0.9 copy-done.9
  84.1 0.8 copy-done.14
  84.9 0.8 copy-done.16
  85.6 5.3 %shard_map.105 = (f32[128,512]{1,0:T(8,128)S(1)}, f32[128,512]{1,0:T(8,128)S(1)}, bf16[128,4096]{1,0:T(8,128)(2,1)S(1)}, bf16[128,4096]{1,0:T(8,128)(2,1)S(1)}) custom-call(s32[3]{0:T(128)S(1)} %pad_add_fusion.meta, bf16[128,8192]{1,0:T(8,128)(2,1)S(1)} %copy-done, bf16[128,8192]{1,0:T(8,128)(2,1)} %collective-permute-done.tok_sib, ...), custom_call_target="tpu_custom_call" | custom-call | flops 2147483648 | bytes 12484608 | tf_op jit(solution)/shard_map/pallas_call | solution.py:25
  90.9 0.1 collective-permute-start.18
  91.0 0.5 collective-permute-start.17
  91.5 2.5 %collective-permute-done.17.other = f32[128,512]{1,0:T(8,128)S(1)} collective-permute-done((f32[128,512]{1,0:T(8,128)S(1)}, f32[128,512]{1,0:T(8,128)S(1)}, u32[]{:S(2)}, u32[]{:S(2)}) %collective-permute-start.17) | collective-permute-done | bytes 262176 | tf_op jit(solution)/shard_map/ppermute | solution.py:254
  94.0 0.0 collective-permute-done.18.grad_other
  94.0 2.1 %shard_map.106 = (bf16[128,512]{1,0:T(8,128)(2,1)}, bf16[128,8192]{1,0:T(8,128)(2,1)}) custom-call(s32[3]{0:T(128)S(1)} %pad_add_fusion.meta, f32[128,512]{1,0:T(8,128)S(1)} %get-tuple-element.33.mine, f32[128,512]{1,0:T(8,128)S(1)} %collective-permute-done.17.other, f32[128,512]{1,0:T(8,128)S(1)} %copy-done.11, ...), custom_call_target="tpu_custom_call" | custom-call | bytes 5111808 | tf_op jit(solution)/shard_map/pallas_call | solution.py:25
  96.1 5.8 %all-to-all-done.1.back = bf16[8,144,512]{2,1,0:T(8,128)(2,1)} async-done(((bf16[8,144,512]{2,1,0:T(8,128)(2,1)}), bf16[8,144,512]{2,1,0:T(8,128)(2,1)}, u32[]{:S(2)}, u32[]{:S(2)}) %all-to-all-start.1) | async-done | bytes 1179680 | tf_op jit(solution)/shard_map/all_to_all | solution.py:262
  102.0 2.3 %shard_map.107 = (bf16[16,64,512]{2,1,0:T(8,128)(2,1)}, bf16[16,2048]{1,0:T(8,128)(2,1)}) custom-call(s32[3]{0:T(128)S(1)} %pad_add_fusion.meta, s32[16]{0:T(128)S(1)} %bitcast.7, bf16[8,144,512]{2,1,0:T(8,128)(2,1)} %all-to-all-done.1.back), custom_call_target="tpu_custom_call" | custom-call | bytes 2293760 | tf_op jit(solution)/shard_map/pallas_call | solution.py:25
  (26 shorter events, 0.0 us)
Async XLA Ops:
  0.6 21.0 %collective-permute-start = (bf16[128,8192]{1,0:T(8,128)(2,1)}, bf16[128,8192]{1,0:T(8,128)(2,1)}, u32[]{:S(2)}, u32[]{:S(2)}) collective-permute-start(bf16[128,8192]{1,0:T(8,128)(2,1)} %tok_own.3), channel_id=1, source_target_pairs={{0,1},{1,0},{2,3},{3,2},{4,5},{5,4},{6,7},{7,6},{8,9},{9,8},{10,11... | collective-permute-start | bytes 6291464 | tf_op jit(solution)/shard_map/ppermute | solution.py:254
  1.1 19.7 %collective-permute-start.3 = (bf16[512,512]{1,0:T(8,128)(2,1)}, bf16[512,512]{1,0:T(8,128)(2,1)S(1)}, u32[]{:S(2)}, u32[]{:S(2)}) collective-permute-start(bf16[512,512]{1,0:T(8,128)(2,1)} %refs_0_.1), channel_id=1, source_target_pairs={{0,2},{1,3},{2,0},{3,1},{4,6},{5,7},{6,4},{7,5},{8,10},{9,11},{10,... | collective-permute-start | bytes 1572872 | tf_op jit(solution)/shard_map/ppermute | solution.py:254
  4.7 11.2 %collective-permute-start.5 = (bf16[256,512]{1,0:T(8,128)(2,1)S(1)}, bf16[256,512]{1,0:T(8,128)(2,1)}, u32[]{:S(2)}, u32[]{:S(2)}) collective-permute-start(bf16[256,512]{1,0:T(8,128)(2,1)S(1)} %constant_dynamic-slice_fusion), channel_id=1, source_target_pairs={{0,12},{1,13},{2,14},{3,15},{4,8},{5,9},{6,10},{7,11},{8,4},{9,5},... | collective-permute-start | bytes 786440 | tf_op jit(solution)/shard_map/ppermute | solution.py:254
  8.4 12.5 %collective-permute-start.4 = (bf16[256,512]{1,0:T(8,128)(2,1)S(1)}, bf16[256,512]{1,0:T(8,128)(2,1)}, u32[]{:S(2)}, u32[]{:S(2)}) collective-permute-start(bf16[256,512]{1,0:T(8,128)(2,1)S(1)} %constant_dynamic-slice_fusion), channel_id=1, source_target_pairs={{0,4},{1,5},{2,6},{3,7},{4,0},{5,1},{6,2},{7,3},{8,12},{9,13},{10,... | collective-permute-start | bytes 786440 | tf_op jit(solution)/shard_map/ppermute | solution.py:254
  8.4 1.5 %collective-permute-start.2 = (bf16[16,2048]{1,0:T(8,128)(2,1)}, bf16[16,2048]{1,0:T(8,128)(2,1)S(1)}, u32[]{:S(2)}, u32[]{:S(2)}) collective-permute-start(bf16[16,2048]{1,0:T(8,128)(2,1)} %up_own.1), channel_id=1, source_target_pairs={{0,1},{1,0},{2,3},{3,2},{4,5},{5,4},{6,7},{7,6},{8,9},{9,8},{10,11... | collective-permute-start | bytes 196616 | tf_op jit(solution)/shard_map/ppermute | solution.py:254
  9.9 5.0 %collective-permute-start.1 = (bf16[128,512]{1,0:T(8,128)(2,1)}, bf16[128,512]{1,0:T(8,128)(2,1)S(1)}, u32[]{:S(2)}, u32[]{:S(2)}) collective-permute-start(bf16[128,512]{1,0:T(8,128)(2,1)} %og_own.4), channel_id=1, source_target_pairs={{0,1},{1,0},{2,3},{3,2},{4,5},{5,4},{6,7},{7,6},{8,9},{9,8},{10,11... | collective-permute-start | bytes 393224 | tf_op jit(solution)/shard_map/ppermute | solution.py:254
  10.1 1.2 %copy-start.5 = (bf16[16,64,512]{2,1,0:T(8,128)(2,1)S(1)}, bf16[16,64,512]{2,1,0:T(8,128)(2,1)}, u32[]{:S(2)}) copy-start(bf16[16,64,512]{2,1,0:T(8,128)(2,1)} %down.1) | copy-start | bytes 3145732
  11.3 0.8 copy-start.12
  12.2 0.7 copy-start.17
  13.8 1.0 copy-start.1
  14.8 39.8 %copy-start = (bf16[128,8192]{1,0:T(8,128)(2,1)S(1)}, bf16[128,8192]{1,0:T(8,128)(2,1)}, u32[]{:S(2)}) copy-start(bf16[128,8192]{1,0:T(8,128)(2,1)} %tok_own.3) | copy-start | bytes 6291460
  14.9 39.8 %copy-start.3 = (bf16[128,512]{1,0:T(8,128)(2,1)S(1)}, bf16[128,512]{1,0:T(8,128)(2,1)}, u32[]{:S(2)}) copy-start(bf16[128,512]{1,0:T(8,128)(2,1)} %og_own.4) | copy-start | bytes 393220
  14.9 39.8 %copy-start.18 = (s32[16,1]{0,1:T(1,128)S(1)}, s32[16,1]{0,1:T(1,128)}, u32[]{:S(2)}) copy-start(s32[16,1]{0,1:T(1,128)} %param.13) | copy-start | bytes 196
  14.9 39.8 %copy-start.19 = (s32[16]{0:T(128)S(1)}, s32[16]{0:T(128)}, u32[]{:S(2)}) copy-start(s32[16]{0:T(128)} %ranks.3) | copy-start | bytes 196
  20.9 0.8 copy-start.6
  21.7 33.0 %all-to-all-start = ((bf16[8,144,512]{2,1,0:T(8,128)(2,1)}), bf16[8,144,512]{2,1,0:T(8,128)(2,1)S(1)}, u32[]{:S(2)}, u32[]{:S(2)}) async-start(bf16[8,144,512]{2,1,0:T(8,128)(2,1)} %copy-done.1), calls=%async_computation | async-start | bytes 2359296 | tf_op jit(solution)/shard_map/all_to_all | solution.py:262
  25.2 21.5 %collective-permute-start.11 = (bf16[256,512]{1,0:T(8,128)(2,1)}, bf16[256,512]{1,0:T(8,128)(2,1)}, u32[]{:S(2)}, u32[]{:S(2)}) collective-permute-start(bf16[256,512]{1,0:T(8,128)(2,1)} %collective-permute-done.5.refs_6_), channel_id=1, source_target_pairs={{0,2},{1,3},{2,0},{3,1},{4,6},{5,7},{6,4},{7,5},{8,10},{9,11},{10,... | collective-permute-start | bytes 786440 | tf_op jit(solution)/shard_map/ppermute | solution.py:254
  27.2 24.8 %collective-permute-start.8 = (bf16[256,512]{1,0:T(8,128)(2,1)}, bf16[256,512]{1,0:T(8,128)(2,1)}, u32[]{:S(2)}, u32[]{:S(2)}) collective-permute-start(bf16[256,512]{1,0:T(8,128)(2,1)} %collective-permute-done.4.refs_2_), channel_id=1, source_target_pairs={{0,2},{1,3},{2,0},{3,1},{4,6},{5,7},{6,4},{7,5},{8,10},{9,11},{10,... | collective-permute-start | bytes 786440 | tf_op jit(solution)/shard_map/ppermute | solution.py:254
  27.3 26.1 %collective-permute-start.13 = (bf16[256,512]{1,0:T(8,128)(2,1)}, bf16[256,512]{1,0:T(8,128)(2,1)}, u32[]{:S(2)}, u32[]{:S(2)}) collective-permute-start(bf16[256,512]{1,0:T(8,128)(2,1)} %collective-permute-done.5.refs_6_), channel_id=1, source_target_pairs={{0,4},{1,5},{2,6},{3,7},{4,0},{5,1},{6,2},{7,3},{8,12},{9,13},{10,... | collective-permute-start | bytes 786440 | tf_op jit(solution)/shard_map/ppermute | solution.py:254
  29.2 24.2 %collective-permute-start.10 = (bf16[256,512]{1,0:T(8,128)(2,1)}, bf16[256,512]{1,0:T(8,128)(2,1)S(1)}, u32[]{:S(2)}, u32[]{:S(2)}) collective-permute-start(bf16[256,512]{1,0:T(8,128)(2,1)} %collective-permute-done.5.refs_6_), channel_id=1, source_target_pairs={{0,16},{1,17},{2,18},{3,19},{4,20},{5,21},{6,22},{7,23},{8,24},{9,... | collective-permute-start | bytes 786440 | tf_op jit(solution)/shard_map/ppermute | solution.py:254
  30.7 29.5 %collective-permute-start.7 = (bf16[256,512]{1,0:T(8,128)(2,1)}, bf16[256,512]{1,0:T(8,128)(2,1)}, u32[]{:S(2)}, u32[]{:S(2)}) collective-permute-start(bf16[256,512]{1,0:T(8,128)(2,1)} %collective-permute-done.4.refs_2_), channel_id=1, source_target_pairs={{0,16},{1,17},{2,18},{3,19},{4,20},{5,21},{6,22},{7,23},{8,24},{9,... | collective-permute-start | bytes 786440 | tf_op jit(solution)/shard_map/ppermute | solution.py:254
  46.7 13.5 %collective-permute-start.12 = (bf16[256,512]{1,0:T(8,128)(2,1)}, bf16[256,512]{1,0:T(8,128)(2,1)}, u32[]{:S(2)}, u32[]{:S(2)}) collective-permute-start(bf16[256,512]{1,0:T(8,128)(2,1)} %collective-permute-done.11.refs_8_), channel_id=1, source_target_pairs={{0,16},{1,17},{2,18},{3,19},{4,20},{5,21},{6,22},{7,23},{8,24},{9,... | collective-permute-start | bytes 786440 | tf_op jit(solution)/shard_map/ppermute | solution.py:254
  51.9 9.6 %collective-permute-start.9 = (bf16[256,512]{1,0:T(8,128)(2,1)}, bf16[256,512]{1,0:T(8,128)(2,1)}, u32[]{:S(2)}, u32[]{:S(2)}) collective-permute-start(bf16[256,512]{1,0:T(8,128)(2,1)} %collective-permute-done.8.refs_4_), channel_id=1, source_target_pairs={{0,16},{1,17},{2,18},{3,19},{4,20},{5,21},{6,22},{7,23},{8,24},{9,... | collective-permute-start | bytes 786440 | tf_op jit(solution)/shard_map/ppermute | solution.py:254
  53.4 8.1 %collective-permute-start.15 = (bf16[256,512]{1,0:T(8,128)(2,1)}, bf16[256,512]{1,0:T(8,128)(2,1)}, u32[]{:S(2)}, u32[]{:S(2)}) collective-permute-start(bf16[256,512]{1,0:T(8,128)(2,1)} %collective-permute-done.13.refs_10_), channel_id=1, source_target_pairs={{0,2},{1,3},{2,0},{3,1},{4,6},{5,7},{6,4},{7,5},{8,10},{9,11},{10,... | collective-permute-start | bytes 786440 | tf_op jit(solution)/shard_map/ppermute | solution.py:254
  53.4 0.7 copy-start.8
  54.1 11.1 %collective-permute-start.14 = (bf16[256,512]{1,0:T(8,128)(2,1)}, bf16[256,512]{1,0:T(8,128)(2,1)}, u32[]{:S(2)}, u32[]{:S(2)}) collective-permute-start(bf16[256,512]{1,0:T(8,128)(2,1)} %collective-permute-done.13.refs_10_), channel_id=1, source_target_pairs={{0,16},{1,17},{2,18},{3,19},{4,20},{5,21},{6,22},{7,23},{8,24},{9,... | collective-permute-start | bytes 786440 | tf_op jit(solution)/shard_map/ppermute | solution.py:254
  59.0 0.6 copy-start.13
  59.6 0.6 copy-start.15
  60.2 5.0 %collective-permute-start.6 = (f32[256,64]{1,0:T(8,128)S(1)}, f32[256,64]{1,0:T(8,128)S(1)}, u32[]{:S(2)}, u32[]{:S(2)}) collective-permute-start(f32[256,64]{1,0:T(8,128)S(1)} %get-tuple-element.25.low), channel_id=1, source_target_pairs={{0,1},{1,0},{2,3},{3,2},{4,5},{5,4},{6,7},{7,6},{8,9},{9,8},{10,11... | collective-permute-start | bytes 196616 | tf_op jit(solution)/shard_map/ppermute | solution.py:254
  66.9 1.0 copy-start.2
  67.9 0.7 copy-start.10
  68.6 33.4 %all-to-all-start.1 = ((bf16[8,144,512]{2,1,0:T(8,128)(2,1)}), bf16[8,144,512]{2,1,0:T(8,128)(2,1)}, u32[]{:S(2)}, u32[]{:S(2)}) async-start(bf16[8,144,512]{2,1,0:T(8,128)(2,1)} %copy-done.2), calls=%async_computation.1 | async-start | bytes 2359296 | tf_op jit(solution)/shard_map/all_to_all | solution.py:262
  73.7 7.3 %collective-permute-start.16 = (bf16[256,512]{1,0:T(8,128)(2,1)}, bf16[256,512]{1,0:T(8,128)(2,1)S(1)}, u32[]{:S(2)}, u32[]{:S(2)}) collective-permute-start(bf16[256,512]{1,0:T(8,128)(2,1)} %collective-permute-done.15.refs_12_), channel_id=1, source_target_pairs={{0,16},{1,17},{2,18},{3,19},{4,20},{5,21},{6,22},{7,23},{8,24},{9,... | collective-permute-start | bytes 786440 | tf_op jit(solution)/shard_map/ppermute | solution.py:254
  81.1 1.0 copy-start.4
  82.1 1.0 copy-start.7
  83.1 0.9 copy-start.9
  84.1 0.8 copy-start.14
  84.9 0.8 copy-start.16
  85.6 8.4 %copy-start.11 = (f32[128,512]{1,0:T(8,128)S(1)}, f32[128,512]{1,0:T(8,128)}, u32[]{:S(2)}) copy-start(f32[128,512]{1,0:T(8,128)} %copy-done.10) | copy-start | bytes 786436
  90.9 3.1 %collective-permute-start.18 = (bf16[128,4096]{1,0:T(8,128)(2,1)S(1)}, bf16[128,4096]{1,0:T(8,128)(2,1)S(1)}, u32[]{:S(2)}, u32[]{:S(2)}) collective-permute-start(bf16[128,4096]{1,0:T(8,128)(2,1)S(1)} %get-tuple-element.36), channel_id=1, source_target_pairs={{0,1},{1,0},{2,3},{3,2},{4,5},{5,4},{6,7},{7,6},{8,9},{9,8},{10,11... | collective-permute-start | bytes 3145736 | tf_op jit(solution)/shard_map/ppermute | solution.py:254
  91.0 3.0 %collective-permute-start.17 = (f32[128,512]{1,0:T(8,128)S(1)}, f32[128,512]{1,0:T(8,128)S(1)}, u32[]{:S(2)}, u32[]{:S(2)}) collective-permute-start(f32[128,512]{1,0:T(8,128)S(1)} %get-tuple-element.34), channel_id=1, source_target_pairs={{0,1},{1,0},{2,3},{3,2},{4,5},{5,4},{6,7},{7,6},{8,9},{9,8},{10,11... | collective-permute-start | bytes 786440 | tf_op jit(solution)/shard_map/ppermute | solution.py:254
where the time goes:
time: 105 us; the launch traced here: 104 us
  waiting for transfers between devices  45.9 us (44%)
  starting transfers between devices  27.2 us (26%)
  Pallas kernels  16.6 us (16%)
  local copies, waits for them, and re-layouts  13.7 us (13%)
    ppermute x19, waiting for transfers between devices, send(): return lax.ppermute(x, AXES, pairs(groups, size, to))  40.1 us
    ppermute x19, starting transfers between devices, send(): return lax.ppermute(x, AXES, pairs(groups, size, to))  18.5 us
    pallas_call x5, Pallas kernels, call(): pl.pallas_call(kernel, out_shape=outs, in_specs=[SMEM] * len(scalars) + [...  15 us
    unnamed x40, local copies, waits for them, and re-layouts  12.7 us
    all_to_all x2, starting transfers between devices, exchange(): lax.all_to_all(blocks, 'dp', split_axis=0, concat_axis=0, tiled=True, axi...  8.72 us
    all_to_all x2, waiting for transfers between devices, exchange(): lax.all_to_all(blocks, 'dp', split_axis=0, concat_axis=0, tiled=True, axi...  5.84 us
  transfers between devices with their start and end apart: 21, of which 10 were waited for; matrix products, arithmetic and copies ran while one was open for 1% of the time, Pallas kernels for 12%

commit v1 on v0

--- a/solution.py
+++ b/solution.py
@@ -19,7 +19,7 @@
     return lax.dot_general(a, b, (((ca,), (cb,)), ((), ())), preferred_element_type=F32)
 
 
-def call(kernel, outs, scalars, arrays, flops=0):
+def call(kernel, outs, scalars, arrays, flops=0, room=30):
     size = sum(x.size * x.dtype.itemsize for x in arrays)
     size += sum(x.size * x.dtype.itemsize for x in outs)
     return pl.pallas_call(
@@ -27,7 +27,7 @@
         out_shape=outs,
         in_specs=[SMEM] * len(scalars) + [VMEM] * len(arrays),
         out_specs=[VMEM] * len(outs),
-        compiler_params=pltpu.CompilerParams(vmem_limit_bytes=30 * 1024 * 1024),
+        compiler_params=pltpu.CompilerParams(vmem_limit_bytes=room * 1024 * 1024),
         cost_estimate=pl.CostEstimate(flops=flops, bytes_accessed=size, transcendentals=0),
     )(*scalars, *arrays)
 
@@ -46,27 +46,34 @@
     return jnp.where(iota((1, width), 1) < count * RANK_TILE, scale, 0.0)
 
 
-def pack_kernel(meta, ids, down, up_own, up_other, blocks):
-    adapters, rank, width = down.shape
-    chips = blocks.shape[0]
-    c = meta[1]
-    rows = chips * 16
-    q = iota((rows, adapters), 0)
-    chosen = jnp.zeros((rows, adapters), jnp.int32)
-    for chip in range(chips):
+def ids_of(ids, n, per, q):
+    out = jnp.zeros(q.shape, jnp.int32)
+    for i in range(n):
+        out = jnp.where(q // per == i, ids[i], out)
+    return out
+
+
+def onehot(mask):
+    return mask.astype(F32).astype(BF16)
+
+
+def up_pack_kernel(ids, up, blocks):
+    tiles, rows, lanes = blocks.shape
+    q = iota((tiles * rows, up.shape[0]), 0)
+    match = ids_of(ids, tiles, rows, q) == iota(q.shape, 1)
+    packed = jnp.zeros((tiles * rows, lanes), F32)
+    for r in range(rows):
+        pick = onehot(match & (q % rows == r))
+        packed = packed + dot(pick, up[:, lanes * r : lanes * (r + 1)], 1, 0)
+    blocks[...] = packed.astype(BF16).reshape(blocks.shape)
+
+
+def pack_kernel(meta, ids, down, blocks):
+    rank = down.shape[1]
+    for chip in range(blocks.shape[0]):
         for slot in range(2):
-            adapter = ids[2 * chip + jnp.bitwise_xor(c, slot)]
+            adapter = ids[2 * chip + jnp.bitwise_xor(meta[1], slot)]
             blocks[chip, rank * slot : rank * (slot + 1), :] = down[adapter]
-            chosen = jnp.where(q // 8 == 2 * chip + slot, adapter, chosen)
-    match = chosen == iota((rows, adapters), 1)
-    packed = jnp.zeros((rows, width), F32)
-    for side, up in enumerate((up_own, up_other)):
-        for r in range(4):
-            pick = (match & (q % 8 == 4 * side + r)).astype(F32).astype(BF16)
-            packed = packed + dot(pick, up[:, width * r : width * (r + 1)], 1, 0)
-    packed = packed.astype(BF16)
-    for chip in range(chips):
-        blocks[chip, 2 * rank : 2 * rank + 16, :] = packed[16 * chip : 16 * (chip + 1), :]
 
 
 def lane_masks(out_width, width, rank):
@@ -76,41 +83,42 @@
     return lane_ok, fold
 
 
-def rank_kernel(
-    meta, ids, ranks, tok_own, tok_sib, og_own, og_sib, blocks, grads, low, back_own, back_sib, up_out
-):
+def backward_kernel(meta, ids, ranks, og, packed, up_out, back):
+    tiles, rows, lanes = packed.shape
+    out_width = og.shape[1]
+    rank = back.shape[1]
+    flat = packed[...].reshape(tiles * rows, lanes)
+    lane_ok, fold = lane_masks(out_width, lanes, rank)
+    q = iota((out_width, tiles * rows), 1)
+    pick = onehot(iota(q.shape, 0) // (lanes // rank) == q)
+    spread = jnp.where(lane_ok, dot(pick, flat, 1, 0), 0.0).astype(BF16)
+    up = dot(spread, fold, 1, 0).astype(BF16)
+    up_out[...] = up
+    factor = factor_of(ids, ranks, 2 * meta[0] + meta[1], rank)
+    back[...] = (dot(og[...], up, 1, 0) * factor).astype(BF16)
+
+
+def grad_kernel(meta, tok_own, tok_sib, back_own, back_sib, grads_own, grads_sib):
+    chips, rank, width = grads_own.shape
+    pairs_of = ((tok_own, back_own, grads_own), (tok_sib, back_sib, grads_sib))
+    for tok, back, grads in pairs_of:
+        turned = back[...].T
+        for i in range(chips):
+            start = pl.multiple_of((2 * i + meta[1]) * width, width)
+            term = dot(turned, tok[:, pl.ds(start, width)], 1, 0)
+            grads[i, 0:rank, :] = term.astype(BF16)
+
+
+def low_kernel(meta, tok_own, tok_sib, blocks, low):
     chips, _, width = blocks.shape
     rows = tok_own.shape[0]
-    out_width = og_own.shape[1]
-    rank = back_own.shape[1]
-    k, c = meta[0], meta[1]
-    heads = out_width // (2 * chips)
-    per_row = width // rank
-    packed = jnp.concatenate([blocks[i, 2 * rank : 2 * rank + 16, :] for i in range(chips)], axis=0)
-    q = iota((out_width, chips * 16), 1)
-    o = iota((out_width, chips * 16), 0)
-    device = 2 * (q // 16) + jnp.bitwise_xor(c, (q // 4) % 2)
-    place = o // per_row == device * (heads // per_row) + q % 4
-    lane_ok, fold = lane_masks(out_width, width, rank)
-    for slot, (tok, og, back) in enumerate(
-        ((tok_own, og_own, back_own), (tok_sib, og_sib, back_sib))
-    ):
-        pick = (place & ((q // 8) % 2 == slot)).astype(F32).astype(BF16)
-        spread = jnp.where(lane_ok, dot(pick, packed, 1, 0), 0.0).astype(BF16)
-        up = dot(spread, fold, 1, 0).astype(BF16)
-        if slot == 0:
-            up_out[...] = up
-        factor = factor_of(ids, ranks, 2 * k + jnp.bitwise_xor(c, slot), rank)
-        backward = (dot(og[...], up, 1, 0) * factor).astype(BF16)
-        back[...] = backward
-        turned = backward.T
+    rank = low.shape[1]
+    for slot, tok in enumerate((tok_own, tok_sib)):
         total = jnp.zeros((rows, rank), F32)
-        half = slice(rank * slot, rank * (slot + 1))
         for i in range(chips):
-            start = pl.multiple_of((2 * i + c) * width, width)
+            start = pl.multiple_of((2 * i + meta[1]) * width, width)
             part = tok[:, pl.ds(start, width)]
-            grads[i, half, :] = dot(turned, part, 1, 0).astype(BF16)
-            total = total + dot(part, blocks[i, half, :], 1, 1)
+            total = total + dot(part, blocks[i, rank * slot : rank * (slot + 1), :], 1, 1)
         low[rows * slot : rows * (slot + 1), :] = total
 
 
@@ -134,7 +142,7 @@
             out_low[...] = dot(hidden, up[...], 1, 1)
         term = dot(og[...], hidden, 0, 0).astype(BF16)
         spread = jnp.where(lane_ok, dot(term, fold, 1, 1), 0.0).astype(BF16)
-        pick = (place & ((q // 4) % 4 == slot)).astype(F32).astype(BF16)
+        pick = onehot(place & ((q // 4) % 4 == slot))
         packed = packed + dot(pick, spread, 1, 0)
     terms[...] = packed.astype(BF16).reshape(terms.shape)
 
@@ -184,21 +192,21 @@
         grad_in[:, pl.ds(sib, width)] = grad_other[:, cols]
 
 
-def back_kernel(meta, ids, back, down_out, up_out):
+def back_kernel(meta, ids, first, second, down_out, up_out):
     rank = down_out.shape[1]
-    chips, _, width = back.shape
+    chips, _, width = first.shape
     c = meta[1]
-    flat = jnp.concatenate([back[i, 2 * rank : 2 * rank + 16, :] for i in range(chips)], axis=0)
+    flat = jnp.concatenate([second[i, rank : rank + 16, :] for i in range(chips)], axis=0)
     q = iota((up_out.shape[0], chips * 16), 1)
     chosen = jnp.full(q.shape, -1, jnp.int32)
     for chip in range(chips):
-        for slot in range(2):
+        for slot, back in enumerate((first, second)):
             adapter = ids[2 * chip + jnp.bitwise_xor(c, slot)]
-            down_out[adapter] = back[chip, rank * slot : rank * (slot + 1), :]
+            down_out[adapter] = back[chip, 0:rank, :]
             chosen = jnp.where(q // 4 == 4 * chip + slot, adapter, chosen)
     match = chosen == iota(q.shape, 0)
     for r in range(4):
-        pick = (match & (q % 4 == r)).astype(F32).astype(BF16)
+        pick = onehot(match & (q % 4 == r))
         up_out[:, width * r : width * (r + 1)] = dot(pick, flat, 1, 0).astype(BF16)
 
 
@@ -216,7 +224,7 @@
     return out
 
 
-def gather_weight(weight, groups, size, send, packed):
+def gather_weight(weight, groups, size, send, ready):
     chips = size // 2
     rows = weight.shape[0]
     if groups != 2 or chips != 8:
@@ -229,8 +237,8 @@
     swap_y = lambda g, d: (g, d ^ 2)
     far = send(mine, lambda g, d: (g, d ^ 12))
     near = send(mine, lambda g, d: (g, d ^ 4))
-    own_y = send(weight, swap_y)
-    far_near = send(after(far, packed), lambda g, d: (g, d ^ 4))
+    own_y = send(after(weight, mine), swap_y)
+    far_near = send(after(far, *ready), lambda g, d: (g, d ^ 4))
     arrays = [weight, own_y]
     plan = [(0, 0, rows, None), (1, 1, rows, None)]
     for j, held in ((2, near), (6, far), (4, far_near)):
@@ -238,7 +246,7 @@
         first = len(arrays)
         arrays += [held, send(held, swap_x), over_y, send(over_y, swap_x)]
         plan += [(first + i, j + i // 2, half, i % 2) for i in range(4)]
-    return arrays, plan, (own_y, near, far), arrays[:-1]
+    return arrays, plan, (own_y, near, far), (arrays[4], arrays[8], arrays[12], arrays[3], arrays[7], arrays[9])
 
 
 def body(groups, size, tokens, out_grad, base_weight, adapter_down, adapter_up, rank_tiles, tile_adapter):
@@ -263,42 +271,50 @@
             blocks, "dp", split_axis=0, concat_axis=0, tiled=True, axis_index_groups=same_core
         )
 
-    up_sib = sibling(adapter_up)
     tok_sib = sibling(tokens)
     og_sib = sibling(out_grad)
-    (packed,) = call(
-        pack_kernel,
-        [shape((chips, 2 * rank + 16, width))],
-        (meta, ids),
-        (adapter_down, adapter_up, up_sib),
-    )
-    weights, plan, first, early = gather_weight(base_weight, groups, size, send, packed)
-    blocks = exchange(after(packed, tok_sib, og_sib, *first))
-
-    grads, low, back_own, back_sib, up_mine = call(
-        rank_kernel,
-        [
-            shape((chips, 2 * rank + 16, width)),
-            shape((2 * rows, rank), F32),
-            shape((rows, rank)),
-            shape((rows, rank)),
-            shape((out_width, rank)),
-        ],
+    up_rows = adapter_up.shape[1] // 128
+    (up_packed,) = call(up_pack_kernel, [shape((size, up_rows, 128))], (ids,), (adapter_up,))
+    up_parts = lax.all_to_all(up_packed, "dp", split_axis=0, concat_axis=0, tiled=True)
+    up_mine, back_own = call(
+        backward_kernel,
+        [shape((out_width, rank)), shape((rows, rank))],
         (meta, ids, rank_tiles),
-        (tokens, tok_sib, out_grad, og_sib, blocks),
-        flops=4 * rows * model_width * rank,
-    )
-    size_up = pl.BlockSpec((chips, 16, width), lambda i: (0, rank // 8, 0))
-    out_low, grads = pl.pallas_call(
+        (out_grad, up_parts),
+    )
+    back_sib = sibling(back_own)
+    grads_own, grads_sib = call(
+        grad_kernel,
+        [shape((chips, rank, width)), shape((chips, rank + 16, width))],
+        (meta,),
+        (tokens, tok_sib, back_own, back_sib),
+        flops=2 * rows * model_width * rank,
+    )
+
+    (packed,) = call(pack_kernel, [shape((chips, 2 * rank, width))], (meta, ids), (adapter_down,))
+    weights, plan, first, early = gather_weight(
+        base_weight, groups, size, send, (packed, up_parts)
+    )
+    blocks = exchange(after(packed, up_parts, tok_sib, og_sib, *first))
+    first_back = exchange(after(grads_own, blocks, *early))
+    (low,) = call(
+        low_kernel,
+        [shape((2 * rows, rank), F32)],
+        (meta,),
+        (tokens, tok_sib, blocks),
+        flops=2 * rows * model_width * rank,
+    )
+    size_up = pl.BlockSpec((chips, 16, width), lambda i: (0, rank // 16, 0))
+    out_low, grads_sib = pl.pallas_call(
         hidden_kernel,
         grid=(1,),
-        out_shape=[shape((rows, out_width), F32), shape(grads.shape)],
+        out_shape=[shape((rows, out_width), F32), shape(grads_sib.shape)],
         in_specs=[SMEM] * 3 + [VMEM] * 5 + [pl.BlockSpec(memory_space=pl.ANY)],
         out_specs=[pl.BlockSpec((rows, out_width), lambda i: (0, 0)), size_up],
         input_output_aliases={8: 1},
         compiler_params=pltpu.CompilerParams(vmem_limit_bytes=30 * 1024 * 1024),
-    )(meta, ids, rank_tiles, low, sibling(low), after(out_grad, *early), og_sib, up_mine, grads)
-    grads_back = exchange(grads)
+    )(meta, ids, rank_tiles, low, sibling(low), out_grad, og_sib, up_mine, grads_sib)
+    second_back = exchange(after(grads_sib, first_back))
 
     for_own, for_sib, grad_own, grad_sib = call(
         functools.partial(base_kernel, plan),
@@ -306,6 +322,7 @@
         (meta,),
         (tokens, tok_sib, out_grad, og_sib, after(back_own, out_low), back_sib, blocks, *weights),
         flops=4 * rows * model_width * out_width,
+        room=60,
     )
     for_other, grad_other = sibling(for_sib), sibling(grad_sib)
     result, grad_in = call(
@@ -318,7 +335,7 @@
         back_kernel,
         [shape(adapter_down.shape), shape(adapter_up.shape)],
         (meta, ids),
-        (grads_back,),
+        (first_back, second_back),
     )
     return result, grad_in, down_grad, up_grad
 

time: 105 us -> 102 us (0.971)
  waiting for transfers between devices: 45.9 us -> 28.6 us
  starting transfers between devices: 27.2 us -> 37.9 us
  Pallas kernels: 16.6 us -> 21.5 us
  local copies, waits for them, and re-layouts: 13.7 us -> 12.2 us
    ppermute x19, waiting for transfers between devices: 40.1 us -> 22 us  [send(): return lax.ppermute(x, AXES, pairs(groups, size, to))]
    all_to_all x2 -> x3, starting transfers between devices: 8.72 us -> 14.7 us  [exchange(): lax.all_to_all(blocks, 'dp', split_axis=0, concat_axis=0, tiled=True, axi...]
    pallas_call x5 -> x8, Pallas kernels: 15 us -> 20 us  [call(): pl.pallas_call(kernel, out_shape=outs, in_specs=[SMEM] * len(scalars) + [...]
    all_to_all x0 -> x1, starting transfers between devices: none -> 3.52 us  [body(): lax.all_to_all(up_packed, 'dp', split_axis=0, concat_axis=0, tiled=True)]
    all_to_all x0 -> x1, waiting for transfers between devices: none -> 3.29 us  [body(): lax.all_to_all(up_packed, 'dp', split_axis=0, concat_axis=0, tiled=True)]
    all_to_all x2 -> x3, waiting for transfers between devices: 5.84 us -> 3.31 us  [exchange(): lax.all_to_all(blocks, 'dp', split_axis=0, concat_axis=0, tiled=True, axi...]
    unnamed x40 -> x62, local copies, waits for them, and re-layouts: 12.7 us -> 11.2 us
    ppermute x19, starting transfers between devices: 18.5 us -> 19.7 us  [send(): return lax.ppermute(x, AXES, pairs(groups, size, to))]
  transfers between devices with their start and end apart: 21 -> 23, of which waited for: 10 -> 7; matrix products, arithmetic and copies ran while one was open for 1% -> 1% of each run, Pallas kernels for 12% -> 19%
where the time goes in v1:
time: 102 us; the launch traced here: 101 us
  starting transfers between devices  37.9 us (37%)
  waiting for transfers between devices  28.6 us (28%)
  Pallas kernels  21.5 us (21%)
  local copies, waits for them, and re-layouts  12.2 us (12%)
    ppermute x19, waiting for transfers between devices, send(): return lax.ppermute(x, AXES, pairs(groups, size, to))  22 us
    pallas_call x8, Pallas kernels, call(): pl.pallas_call(kernel, out_shape=outs, in_specs=[SMEM] * len(scalars) + [...  20 us
    ppermute x19, starting transfers between devices, send(): return lax.ppermute(x, AXES, pairs(groups, size, to))  19.7 us
    all_to_all x3, starting transfers between devices, exchange(): lax.all_to_all(blocks, 'dp', split_axis=0, concat_axis=0, tiled=True, axi...  14.7 us
    unnamed x62, local copies, waits for them, and re-layouts  11.2 us
    all_to_all x1, starting transfers between devices, body(): lax.all_to_all(up_packed, 'dp', split_axis=0, concat_axis=0, tiled=True)  3.52 us
    all_to_all x3, waiting for transfers between devices, exchange(): lax.all_to_all(blocks, 'dp', split_axis=0, concat_axis=0, tiled=True, axi...  3.31 us
    all_to_all x1, waiting for transfers between devices, body(): lax.all_to_all(up_packed, 'dp', split_axis=0, concat_axis=0, tiled=True)  3.29 us
  transfers between devices with their start and end apart: 23, of which 7 were waited for; matrix products, arithmetic and copies ran while one was open for 1% of the time, Pallas kernels for 19%

profile of v1, /device:TPU:0, one launch (start us, length us, event | category | flops | bytes accessed | tf_op | source)
XLA Modules:
  0.0 101.3 jit_solution(7246686527083936933)
XLA Ops:
  0.6 0.5 collective-permute-start
  1.1 1.0 constant_dynamic-slice_fusion
  2.1 2.6 %collective-permute-start.2 = (bf16[512,512]{1,0:T(8,128)(2,1)}, bf16[512,512]{1,0:T(8,128)(2,1)S(1)}, u32[]{:S(2)}, u32[]{:S(2)}) collective-permute-start(bf16[512,512]{1,0:T(8,128)(2,1)} %refs_0_.1), channel_id=1, source_target_pairs={{0,2},{1,3},{2,0},{3,1},{4,6},{5,7},{6,4},{7,5},{8,10},{9,11},{10,... | collective-permute-start | bytes 1572872 | tf_op jit(solution)/shard_map/ppermute | solution.py:262
  4.7 3.6 %collective-permute-start.4 = (bf16[256,512]{1,0:T(8,128)(2,1)S(1)}, bf16[256,512]{1,0:T(8,128)(2,1)}, u32[]{:S(2)}, u32[]{:S(2)}) collective-permute-start(bf16[256,512]{1,0:T(8,128)(2,1)S(1)} %constant_dynamic-slice_fusion), channel_id=1, source_target_pairs={{0,12},{1,13},{2,14},{3,15},{4,8},{5,9},{6,10},{7,11},{8,4},{9,5},... | collective-permute-start | bytes 786440 | tf_op jit(solution)/shard_map/ppermute | solution.py:262
  8.3 0.0 collective-permute-start.3
  8.3 0.8 copy-done.16
  9.2 0.7 copy-done.19
  9.8 1.6 %shard_map.102 = bf16[16,16,128]{2,1,0:T(8,128)(2,1)} custom-call(s32[16]{0:T(128)S(1)} %bitcast.4, bf16[16,2048]{1,0:T(8,128)(2,1)S(1)} %copy-done.16), custom_call_target="tpu_custom_call" | custom-call | bytes 131072 | tf_op jit(solution)/shard_map/pallas_call | solution.py:25
  11.4 3.5 %all-to-all-start = ((bf16[16,16,128]{2,1,0:T(8,128)(2,1)}), bf16[16,16,128]{2,1,0:T(8,128)(2,1)S(1)}, u32[]{:S(2)}, u32[]{:S(2)}) async-start(bf16[16,16,128]{2,1,0:T(8,128)(2,1)} %shard_map.102), calls=%async_computation | async-start | bytes 131072 | tf_op jit(solution)/shard_map/all_to_all | solution.py:278
  15.0 0.1 pad_add_fusion.meta
  15.0 1.2 %copy-done.8 = bf16[16,64,512]{2,1,0:T(8,128)(2,1)S(1)} copy-done((bf16[16,64,512]{2,1,0:T(8,128)(2,1)S(1)}, bf16[16,64,512]{2,1,0:T(8,128)(2,1)}, u32[]{:S(2)}) %copy-start.8) | copy-done | bytes 1048600
  16.3 0.7 copy-done.20
  16.9 0.0 copy-start
  16.9 0.6 shard_map.104
  17.6 0.0 copy-start.2
  17.6 1.0 copy-done.2
  18.5 3.3 %all-to-all-done.packed = bf16[16,16,128]{2,1,0:T(8,128)(2,1)S(1)} async-done(((bf16[16,16,128]{2,1,0:T(8,128)(2,1)}), bf16[16,16,128]{2,1,0:T(8,128)(2,1)S(1)}, u32[]{:S(2)}, u32[]{:S(2)}) %all-to-all-start) | async-done | bytes 65568 | tf_op jit(solution)/shard_map/all_to_all | solution.py:278
  21.8 0.0 collective-permute-done.1.og_sib
  21.8 0.0 collective-permute-done.4.refs_6_
  21.8 0.0 collective-permute-done.3.refs_2_
  21.9 0.0 collective-permute-done.2.refs_1_
  21.9 0.7 copy-done.24
  22.6 0.2 copy-done.23
  22.8 5.3 %all-to-all-start.1 = ((bf16[8,128,512]{2,1,0:T(8,128)(2,1)}), bf16[8,128,512]{2,1,0:T(8,128)(2,1)S(1)}, u32[]{:S(2)}, u32[]{:S(2)}) async-start(bf16[8,128,512]{2,1,0:T(8,128)(2,1)} %copy-done.2), calls=%async_computation.1 | async-start | bytes 2097152 | tf_op jit(solution)/shard_map/all_to_all | solution.py:270
  28.1 2.0 %collective-permute-start.13 = (bf16[256,512]{1,0:T(8,128)(2,1)}, bf16[256,512]{1,0:T(8,128)(2,1)S(1)}, u32[]{:S(2)}, u32[]{:S(2)}) collective-permute-start(bf16[256,512]{1,0:T(8,128)(2,1)} %collective-permute-done.4.refs_6_), channel_id=1, source_target_pairs={{0,4},{1,5},{2,6},{3,7},{4,0},{5,1},{6,2},{7,3},{8,12},{9,13},{10,... | collective-permute-start | bytes 786440 | tf_op jit(solution)/shard_map/ppermute | solution.py:262
  30.1 1.5 %collective-permute-start.11 = (bf16[256,512]{1,0:T(8,128)(2,1)}, bf16[256,512]{1,0:T(8,128)(2,1)S(1)}, u32[]{:S(2)}, u32[]{:S(2)}) collective-permute-start(bf16[256,512]{1,0:T(8,128)(2,1)} %collective-permute-done.4.refs_6_), channel_id=1, source_target_pairs={{0,2},{1,3},{2,0},{3,1},{4,6},{5,7},{6,4},{7,5},{8,10},{9,11},{10,... | collective-permute-start | bytes 786440 | tf_op jit(solution)/shard_map/ppermute | solution.py:262
  31.6 1.1 %shard_map.103 = (bf16[512,64]{1,0:T(8,128)(2,1)S(1)}, bf16[128,64]{1,0:T(8,128)(2,1)S(1)}) custom-call(s32[3]{0:T(128)S(1)} %pad_add_fusion.meta, s32[16]{0:T(128)S(1)} %bitcast.6, s32[16]{0:T(128)S(1)} %copy-done.22, bf16[128,512]{1,0:T(8,128)(2,1)S(1)} %copy-done.6, bf16[16,16,128]{2,1,0:T(8,128)(2,1)S(1)} %all-to-all-done.packed), custom_call_target="tpu_custom_call" | custom-call | bytes 278528 | tf_op jit(solution)/shard_map/pallas_call | solution.py:25
  32.7 0.6 copy-done.14
  33.3 0.0 collective-permute-start.6
  33.4 1.5 %collective-permute-start.10 = (bf16[256,512]{1,0:T(8,128)(2,1)}, bf16[256,512]{1,0:T(8,128)(2,1)S(1)}, u32[]{:S(2)}, u32[]{:S(2)}) collective-permute-start(bf16[256,512]{1,0:T(8,128)(2,1)} %collective-permute-done.4.refs_6_), channel_id=1, source_target_pairs={{0,16},{1,17},{2,18},{3,19},{4,20},{5,21},{6,22},{7,23},{8,24},{9,... | collective-permute-start | bytes 786440 | tf_op jit(solution)/shard_map/ppermute | solution.py:262
  34.8 0.6 collective-permute-start.8
  35.4 0.6 collective-permute-start.7
  36.1 15.7 %collective-permute-done.13.refs_10_ = bf16[256,512]{1,0:T(8,128)(2,1)S(1)} collective-permute-done((bf16[256,512]{1,0:T(8,128)(2,1)}, bf16[256,512]{1,0:T(8,128)(2,1)S(1)}, u32[]{:S(2)}, u32[]{:S(2)}) %collective-permute-start.13) | collective-permute-done | bytes 262176 | tf_op jit(solution)/shard_map/ppermute | solution.py:262
  51.8 1.1 %collective-permute-start.15 = (bf16[256,512]{1,0:T(8,128)(2,1)S(1)}, bf16[256,512]{1,0:T(8,128)(2,1)S(1)}, u32[]{:S(2)}, u32[]{:S(2)}) collective-permute-start(bf16[256,512]{1,0:T(8,128)(2,1)S(1)} %collective-permute-done.13.refs_10_), channel_id=1, source_target_pairs={{0,2},{1,3},{2,0},{3,1},{4,6},{5,7},{6,4},{7,5},{8,10},{9,11},{10,... | collective-permute-start | bytes 786440 | tf_op jit(solution)/shard_map/ppermute | solution.py:262
  52.9 0.0 collective-permute-done.11.refs_8_
  52.9 1.5 %collective-permute-start.12 = (bf16[256,512]{1,0:T(8,128)(2,1)S(1)}, bf16[256,512]{1,0:T(8,128)(2,1)}, u32[]{:S(2)}, u32[]{:S(2)}) collective-permute-start(bf16[256,512]{1,0:T(8,128)(2,1)S(1)} %collective-permute-done.11.refs_8_), channel_id=1, source_target_pairs={{0,16},{1,17},{2,18},{3,19},{4,20},{5,21},{6,22},{7,23},{8,24},{9,... | collective-permute-start | bytes 786440 | tf_op jit(solution)/shard_map/ppermute | solution.py:262
  54.4 2.1 %shard_map.106 = (bf16[8,64,512]{2,1,0:T(8,128)(2,1)S(1)}, bf16[8,80,512]{2,1,0:T(8,128)(2,1)S(1)}) custom-call(s32[3]{0:T(128)S(1)} %pad_add_fusion.meta, bf16[128,8192]{1,0:T(8,128)(2,1)S(1)} %copy-done, bf16[128,8192]{1,0:T(8,128)(2,1)} %collective-permute-done.tok_sib, bf16[128,64]{1,0:T(8,128)(2,1)S(1)} %get-tuple-element.30.back_own, ...), custom_call_target="tpu_custom_call" | custom-call | flops 134217728 | bytes 5406720 | tf_op jit(solution)/shard_map/pallas_call | solution.py:25
  56.5 0.0 copy-start.3
  56.5 0.8 copy-done.3
  57.4 0.8 copy-done.10
  58.2 0.0 collective-permute-done.10.refs_7_
  58.2 0.0 collective-permute-done.7.refs_3_
  58.2 1.1 %collective-permute-done.15.refs_12_ = bf16[256,512]{1,0:T(8,128)(2,1)S(1)} collective-permute-done((bf16[256,512]{1,0:T(8,128)(2,1)S(1)}, bf16[256,512]{1,0:T(8,128)(2,1)S(1)}, u32[]{:S(2)}, u32[]{:S(2)}) %collective-permute-start.15) | collective-permute-done | bytes 262176 | tf_op jit(solution)/shard_map/ppermute | solution.py:262
  59.3 0.7 copy-done.30
  60.0 5.8 %all-to-all-start.2 = ((bf16[8,64,512]{2,1,0:T(8,128)(2,1)}), bf16[8,64,512]{2,1,0:T(8,128)(2,1)}, u32[]{:S(2)}, u32[]{:S(2)}) async-start(bf16[8,64,512]{2,1,0:T(8,128)(2,1)} %copy-done.10), calls=%async_computation.2 | async-start | bytes 1048576 | tf_op jit(solution)/shard_map/all_to_all | solution.py:270
  65.8 1.6 %collective-permute-start.14 = (bf16[256,512]{1,0:T(8,128)(2,1)}, bf16[256,512]{1,0:T(8,128)(2,1)}, u32[]{:S(2)}, u32[]{:S(2)}) collective-permute-start(bf16[256,512]{1,0:T(8,128)(2,1)} %copy-done.25), channel_id=1, source_target_pairs={{0,16},{1,17},{2,18},{3,19},{4,20},{5,21},{6,22},{7,23},{8,24},{9,... | collective-permute-start | bytes 786440 | tf_op jit(solution)/shard_map/ppermute | solution.py:262
  67.4 0.5 collective-permute-start.9
  67.9 1.5 %collective-permute-start.16 = (bf16[256,512]{1,0:T(8,128)(2,1)}, bf16[256,512]{1,0:T(8,128)(2,1)}, u32[]{:S(2)}, u32[]{:S(2)}) collective-permute-start(bf16[256,512]{1,0:T(8,128)(2,1)} %copy-done.30), channel_id=1, source_target_pairs={{0,16},{1,17},{2,18},{3,19},{4,20},{5,21},{6,22},{7,23},{8,24},{9,... | collective-permute-start | bytes 786440 | tf_op jit(solution)/shard_map/ppermute | solution.py:262
  69.4 2.3 %shard_map.105.low = f32[256,64]{1,0:T(8,128)S(1)} custom-call(s32[3]{0:T(128)S(1)} %pad_add_fusion.meta, bf16[128,8192]{1,0:T(8,128)(2,1)S(1)} %copy-done, bf16[128,8192]{1,0:T(8,128)(2,1)} %collective-permute-done.tok_sib, bf16[8,128,512]{2,1,0:T(8,128)(2,1)S(1)} %all-to-all-done.1.blocks), custom_call_target="tpu_custom_call" | custom-call | flops 134217728 | bytes 5308416 | tf_op jit(solution)/shard_map/pallas_call | solution.py:25
  71.7 0.1 collective-permute-start.5
  71.8 1.3 %collective-permute-done.5.other = f32[256,64]{1,0:T(8,128)S(1)} collective-permute-done((f32[256,64]{1,0:T(8,128)S(1)}, f32[256,64]{1,0:T(8,128)S(1)}, u32[]{:S(2)}, u32[]{:S(2)}) %collective-permute-start.5) | collective-permute-done | bytes 65568 | tf_op jit(solution)/shard_map/ppermute | solution.py:262
  73.1 1.6 %shard_map.107 = (f32[128,512]{1,0:T(8,128)S(1)}, bf16[8,80,512]{2,1,0:T(8,128)(2,1)S(1)}) custom-call(s32[3]{0:T(128)S(1)} %pad_add_fusion.meta, s32[16]{0:T(128)S(1)} %bitcast.7, s32[16]{0:T(128)S(1)} %copy-done.22, f32[256,64]{1,0:T(8,128)S(1)} %shard_map.105.low, f32[256,64]{1,0:T(8,128)S(1)} %collective-permute-done.5.other, ...), custom_call_target="tpu_custom_call", output_to_operand_aliasing={{1}: (8, {})} | custom-call | tf_op jit(solution)/shard_map/pallas_call | solution.py:308
  74.7 0.8 copy-done.5
  75.6 3.3 %all-to-all-done.2.first = bf16[8,64,512]{2,1,0:T(8,128)(2,1)} async-done(((bf16[8,64,512]{2,1,0:T(8,128)(2,1)}), bf16[8,64,512]{2,1,0:T(8,128)(2,1)}, u32[]{:S(2)}, u32[]{:S(2)}) %all-to-all-start.2) | async-done | bytes 524320 | tf_op jit(solution)/shard_map/all_to_all | solution.py:270
  78.9 3.6 %all-to-all-start.3 = ((bf16[8,80,512]{2,1,0:T(8,128)(2,1)}), bf16[8,80,512]{2,1,0:T(8,128)(2,1)S(1)}, u32[]{:S(2)}, u32[]{:S(2)}) async-start(bf16[8,80,512]{2,1,0:T(8,128)(2,1)} %copy-done.5), calls=%async_computation.3 | async-start | bytes 1310720 | tf_op jit(solution)/shard_map/all_to_all | solution.py:270
  82.4 0.0 collective-permute-done.14.refs_11_
  82.5 1.1 %collective-permute-done.16.refs_13_ = bf16[256,512]{1,0:T(8,128)(2,1)} collective-permute-done((bf16[256,512]{1,0:T(8,128)(2,1)}, bf16[256,512]{1,0:T(8,128)(2,1)}, u32[]{:S(2)}, u32[]{:S(2)}) %collective-permute-start.16) | collective-permute-done | bytes 262176 | tf_op jit(solution)/shard_map/ppermute | solution.py:262
  83.6 8.1 %shard_map.108 = (f32[128,512]{1,0:T(8,128)}, f32[128,512]{1,0:T(8,128)}, bf16[128,4096]{1,0:T(8,128)(2,1)}, bf16[128,4096]{1,0:T(8,128)(2,1)}) custom-call(s32[3]{0:T(128)} %copy-done.17, bf16[128,8192]{1,0:T(8,128)(2,1)} %tok_own.5, bf16[128,8192]{1,0:T(8,128)(2,1)} %collective-permute-done.tok_sib, bf16[128,512]{1,0:T(8,128)(2,1)} %og_own.3, ...), custom_call_target="tpu_custom_call" | custom-call | flops 2147483648 | bytes 12353536 | tf_op jit(solution)/shard_map/pallas_call | solution.py:25
  91.7 0.5 collective-permute-start.17
  92.2 2.7 %collective-permute-done.17.other = f32[128,512]{1,0:T(8,128)S(1)} collective-permute-done((f32[128,512]{1,0:T(8,128)}, f32[128,512]{1,0:T(8,128)S(1)}, u32[]{:S(2)}, u32[]{:S(2)}) %collective-permute-start.17) | collective-permute-done | bytes 262176 | tf_op jit(solution)/shard_map/ppermute | solution.py:262
  94.9 1.2 %copy-done.7 = bf16[128,4096]{1,0:T(8,128)(2,1)S(1)} copy-done((bf16[128,4096]{1,0:T(8,128)(2,1)S(1)}, bf16[128,4096]{1,0:T(8,128)(2,1)}, u32[]{:S(2)}) %copy-start.7) | copy-done | bytes 1048600
  96.1 0.9 copy-done.11
  97.1 2.1 %shard_map.109 = (bf16[128,512]{1,0:T(8,128)(2,1)}, bf16[128,8192]{1,0:T(8,128)(2,1)}) custom-call(s32[3]{0:T(128)S(1)} %copy-done.18, f32[128,512]{1,0:T(8,128)S(1)} %copy-done.11, f32[128,512]{1,0:T(8,128)S(1)} %collective-permute-done.17.other, f32[128,512]{1,0:T(8,128)S(1)} %get-tuple-element.29.out_low, bf16[128,4096]{1,0:T(8,128)(2,1)S(1)} %copy-done.7, ...), custom_call_target="tpu_custom_call" | custom-call | bytes 5111808 | tf_op jit(solution)/shard_map/pallas_call | solution.py:25
  99.2 2.1 %shard_map.110 = (bf16[16,64,512]{2,1,0:T(8,128)(2,1)}, bf16[16,2048]{1,0:T(8,128)(2,1)}) custom-call(s32[3]{0:T(128)S(1)} %copy-done.18, s32[16]{0:T(128)S(1)} %bitcast.8, bf16[8,64,512]{2,1,0:T(8,128)(2,1)} %all-to-all-done.2.first, bf16[8,80,512]{2,1,0:T(8,128)(2,1)S(1)} %all-to-all-done.3.second), custom_call_target="tpu_custom_call" | custom-call | bytes 2293760 | tf_op jit(solution)/shard_map/pallas_call | solution.py:25
  (55 shorter events, 0.1 us)
Async XLA Ops:
  0.6 21.3 %collective-permute-start = (bf16[128,8192]{1,0:T(8,128)(2,1)}, bf16[128,8192]{1,0:T(8,128)(2,1)}, u32[]{:S(2)}, u32[]{:S(2)}) collective-permute-start(bf16[128,8192]{1,0:T(8,128)(2,1)} %tok_own.5), channel_id=1, source_target_pairs={{0,1},{1,0},{2,3},{3,2},{4,5},{5,4},{6,7},{7,6},{8,9},{9,8},{10,11... | collective-permute-start | bytes 6291464 | tf_op jit(solution)/shard_map/ppermute | solution.py:262
  2.1 19.8 %collective-permute-start.2 = (bf16[512,512]{1,0:T(8,128)(2,1)}, bf16[512,512]{1,0:T(8,128)(2,1)S(1)}, u32[]{:S(2)}, u32[]{:S(2)}) collective-permute-start(bf16[512,512]{1,0:T(8,128)(2,1)} %refs_0_.1), channel_id=1, source_target_pairs={{0,2},{1,3},{2,0},{3,1},{4,6},{5,7},{6,4},{7,5},{8,10},{9,11},{10,... | collective-permute-start | bytes 1572872 | tf_op jit(solution)/shard_map/ppermute | solution.py:262
  4.7 17.1 %collective-permute-start.4 = (bf16[256,512]{1,0:T(8,128)(2,1)S(1)}, bf16[256,512]{1,0:T(8,128)(2,1)}, u32[]{:S(2)}, u32[]{:S(2)}) collective-permute-start(bf16[256,512]{1,0:T(8,128)(2,1)S(1)} %constant_dynamic-slice_fusion), channel_id=1, source_target_pairs={{0,12},{1,13},{2,14},{3,15},{4,8},{5,9},{6,10},{7,11},{8,4},{9,5},... | collective-permute-start | bytes 786440 | tf_op jit(solution)/shard_map/ppermute | solution.py:262
  8.3 13.5 %collective-permute-start.3 = (bf16[256,512]{1,0:T(8,128)(2,1)S(1)}, bf16[256,512]{1,0:T(8,128)(2,1)S(1)}, u32[]{:S(2)}, u32[]{:S(2)}) collective-permute-start(bf16[256,512]{1,0:T(8,128)(2,1)S(1)} %constant_dynamic-slice_fusion), channel_id=1, source_target_pairs={{0,4},{1,5},{2,6},{3,7},{4,0},{5,1},{6,2},{7,3},{8,12},{9,13},{10,... | collective-permute-start | bytes 786440 | tf_op jit(solution)/shard_map/ppermute | solution.py:262
  8.3 13.5 %collective-permute-start.1 = (bf16[128,512]{1,0:T(8,128)(2,1)}, bf16[128,512]{1,0:T(8,128)(2,1)S(1)}, u32[]{:S(2)}, u32[]{:S(2)}) collective-permute-start(bf16[128,512]{1,0:T(8,128)(2,1)} %og_own.3), channel_id=1, source_target_pairs={{0,1},{1,0},{2,3},{3,2},{4,5},{5,4},{6,7},{7,6},{8,9},{9,8},{10,11... | collective-permute-start | bytes 393224 | tf_op jit(solution)/shard_map/ppermute | solution.py:262
  8.3 0.8 copy-start.16
  9.2 0.7 copy-start.19
  11.4 10.4 %all-to-all-start = ((bf16[16,16,128]{2,1,0:T(8,128)(2,1)}), bf16[16,16,128]{2,1,0:T(8,128)(2,1)S(1)}, u32[]{:S(2)}, u32[]{:S(2)}) async-start(bf16[16,16,128]{2,1,0:T(8,128)(2,1)} %shard_map.102), calls=%async_computation | async-start | bytes 131072 | tf_op jit(solution)/shard_map/all_to_all | solution.py:278
  15.0 1.2 %copy-start.8 = (bf16[16,64,512]{2,1,0:T(8,128)(2,1)S(1)}, bf16[16,64,512]{2,1,0:T(8,128)(2,1)}, u32[]{:S(2)}) copy-start(bf16[16,64,512]{2,1,0:T(8,128)(2,1)} %down.1) | copy-start | bytes 3145732
  16.3 0.7 copy-start.20
  16.9 56.2 %copy-start.17 = (s32[3]{0:T(128)}, s32[3]{0:T(128)S(1)}, u32[]{:S(2)}) copy-start(s32[3]{0:T(128)S(1)} %pad_add_fusion.meta) | copy-start | bytes 40
  16.9 14.7 %copy-start.6 = (bf16[128,512]{1,0:T(8,128)(2,1)S(1)}, bf16[128,512]{1,0:T(8,128)(2,1)}, u32[]{:S(2)}) copy-start(bf16[128,512]{1,0:T(8,128)(2,1)} %og_own.3) | copy-start | bytes 393220
  16.9 14.7 %copy-start.21 = (s32[16,1]{0,1:T(1,128)S(1)}, s32[16,1]{0,1:T(1,128)}, u32[]{:S(2)}) copy-start(s32[16,1]{0,1:T(1,128)} %param.13) | copy-start | bytes 196
  16.9 14.7 %copy-start.22 = (s32[16]{0:T(128)S(1)}, s32[16]{0:T(128)}, u32[]{:S(2)}) copy-start(s32[16]{0:T(128)} %ranks.3) | copy-start | bytes 196
  16.9 37.5 %copy-start = (bf16[128,8192]{1,0:T(8,128)(2,1)S(1)}, bf16[128,8192]{1,0:T(8,128)(2,1)}, u32[]{:S(2)}) copy-start(bf16[128,8192]{1,0:T(8,128)(2,1)} %tok_own.5) | copy-start | bytes 6291460
  17.6 1.0 copy-start.2
  21.8 51.3 %copy-start.9 = (bf16[128,512]{1,0:T(8,128)(2,1)}, bf16[128,512]{1,0:T(8,128)(2,1)S(1)}, u32[]{:S(2)}) copy-start(bf16[128,512]{1,0:T(8,128)(2,1)S(1)} %collective-permute-done.1.og_sib) | copy-start | bytes 393220
  21.9 0.7 copy-start.24
  21.9 0.9 copy-start.23
  22.8 37.2 %all-to-all-start.1 = ((bf16[8,128,512]{2,1,0:T(8,128)(2,1)}), bf16[8,128,512]{2,1,0:T(8,128)(2,1)S(1)}, u32[]{:S(2)}, u32[]{:S(2)}) async-start(bf16[8,128,512]{2,1,0:T(8,128)(2,1)} %copy-done.2), calls=%async_computation.1 | async-start | bytes 2097152 | tf_op jit(solution)/shard_map/all_to_all | solution.py:270
  28.1 23.7 %collective-permute-start.13 = (bf16[256,512]{1,0:T(8,128)(2,1)}, bf16[256,512]{1,0:T(8,128)(2,1)S(1)}, u32[]{:S(2)}, u32[]{:S(2)}) collective-permute-start(bf16[256,512]{1,0:T(8,128)(2,1)} %collective-permute-done.4.refs_6_), channel_id=1, source_target_pairs={{0,4},{1,5},{2,6},{3,7},{4,0},{5,1},{6,2},{7,3},{8,12},{9,13},{10,... | collective-permute-start | bytes 786440 | tf_op jit(solution)/shard_map/ppermute | solution.py:262
  30.1 22.8 %collective-permute-start.11 = (bf16[256,512]{1,0:T(8,128)(2,1)}, bf16[256,512]{1,0:T(8,128)(2,1)S(1)}, u32[]{:S(2)}, u32[]{:S(2)}) collective-permute-start(bf16[256,512]{1,0:T(8,128)(2,1)} %collective-permute-done.4.refs_6_), channel_id=1, source_target_pairs={{0,2},{1,3},{2,0},{3,1},{4,6},{5,7},{6,4},{7,5},{8,10},{9,11},{10,... | collective-permute-start | bytes 786440 | tf_op jit(solution)/shard_map/ppermute | solution.py:262
  32.7 0.6 copy-start.14
  33.3 23.1 %copy-start.12 = (bf16[128,64]{1,0:T(8,128)(2,1)}, bf16[128,64]{1,0:T(8,128)(2,1)S(1)}, u32[]{:S(2)}) copy-start(bf16[128,64]{1,0:T(8,128)(2,1)S(1)} %get-tuple-element.30.back_own) | copy-start | bytes 49156
  33.3 2.1 %collective-permute-start.6 = (bf16[128,64]{1,0:T(8,128)(2,1)S(1)}, bf16[128,64]{1,0:T(8,128)(2,1)S(1)}, u32[]{:S(2)}, u32[]{:S(2)}) collective-permute-start(bf16[128,64]{1,0:T(8,128)(2,1)S(1)} %get-tuple-element.30.back_own), channel_id=1, source_target_pairs={{0,1},{1,0},{2,3},{3,2},{4,5},{5,4},{6,7},{7,6},{8,9},{9,8},{10,11... | collective-permute-start | bytes 49160 | tf_op jit(solution)/shard_map/ppermute | solution.py:262
  33.4 24.8 %collective-permute-start.10 = (bf16[256,512]{1,0:T(8,128)(2,1)}, bf16[256,512]{1,0:T(8,128)(2,1)S(1)}, u32[]{:S(2)}, u32[]{:S(2)}) collective-permute-start(bf16[256,512]{1,0:T(8,128)(2,1)} %collective-permute-done.4.refs_6_), channel_id=1, source_target_pairs={{0,16},{1,17},{2,18},{3,19},{4,20},{5,21},{6,22},{7,23},{8,24},{9,... | collective-permute-start | bytes 786440 | tf_op jit(solution)/shard_map/ppermute | solution.py:262
  34.8 23.3 %collective-permute-start.8 = (bf16[256,512]{1,0:T(8,128)(2,1)}, bf16[256,512]{1,0:T(8,128)(2,1)S(1)}, u32[]{:S(2)}, u32[]{:S(2)}) collective-permute-start(bf16[256,512]{1,0:T(8,128)(2,1)} %copy-done.24), channel_id=1, source_target_pairs={{0,2},{1,3},{2,0},{3,1},{4,6},{5,7},{6,4},{7,5},{8,10},{9,11},{10,... | collective-permute-start | bytes 786440 | tf_op jit(solution)/shard_map/ppermute | solution.py:262
  35.4 21.1 %copy-start.13 = (bf16[128,64]{1,0:T(8,128)(2,1)}, bf16[128,64]{1,0:T(8,128)(2,1)S(1)}, u32[]{:S(2)}) copy-start(bf16[128,64]{1,0:T(8,128)(2,1)S(1)} %collective-permute-done.6.back_sib) | copy-start | bytes 49156
  35.4 22.8 %collective-permute-start.7 = (bf16[256,512]{1,0:T(8,128)(2,1)}, bf16[256,512]{1,0:T(8,128)(2,1)S(1)}, u32[]{:S(2)}, u32[]{:S(2)}) collective-permute-start(bf16[256,512]{1,0:T(8,128)(2,1)} %copy-done.24), channel_id=1, source_target_pairs={{0,16},{1,17},{2,18},{3,19},{4,20},{5,21},{6,22},{7,23},{8,24},{9,... | collective-permute-start | bytes 786440 | tf_op jit(solution)/shard_map/ppermute | solution.py:262
  51.8 4.7 %copy-start.25 = (bf16[256,512]{1,0:T(8,128)(2,1)}, bf16[256,512]{1,0:T(8,128)(2,1)S(1)}, u32[]{:S(2)}) copy-start(bf16[256,512]{1,0:T(8,128)(2,1)S(1)} %collective-permute-done.13.refs_10_) | copy-start | bytes 786436
  51.8 7.5 %collective-permute-start.15 = (bf16[256,512]{1,0:T(8,128)(2,1)S(1)}, bf16[256,512]{1,0:T(8,128)(2,1)S(1)}, u32[]{:S(2)}, u32[]{:S(2)}) collective-permute-start(bf16[256,512]{1,0:T(8,128)(2,1)S(1)} %collective-permute-done.13.refs_10_), channel_id=1, source_target_pairs={{0,2},{1,3},{2,0},{3,1},{4,6},{5,7},{6,4},{7,5},{8,10},{9,11},{10,... | collective-permute-start | bytes 786440 | tf_op jit(solution)/shard_map/ppermute | solution.py:262
  52.9 3.6 %copy-start.26 = (bf16[256,512]{1,0:T(8,128)(2,1)}, bf16[256,512]{1,0:T(8,128)(2,1)S(1)}, u32[]{:S(2)}) copy-start(bf16[256,512]{1,0:T(8,128)(2,1)S(1)} %collective-permute-done.11.refs_8_) | copy-start | bytes 786436
  52.9 7.1 %collective-permute-start.12 = (bf16[256,512]{1,0:T(8,128)(2,1)S(1)}, bf16[256,512]{1,0:T(8,128)(2,1)}, u32[]{:S(2)}, u32[]{:S(2)}) collective-permute-start(bf16[256,512]{1,0:T(8,128)(2,1)S(1)} %collective-permute-done.11.refs_8_), channel_id=1, source_target_pairs={{0,16},{1,17},{2,18},{3,19},{4,20},{5,21},{6,22},{7,23},{8,24},{9,... | collective-permute-start | bytes 786440 | tf_op jit(solution)/shard_map/ppermute | solution.py:262
  56.5 0.8 copy-start.3
  57.4 0.8 copy-start.10
  58.2 1.1 %copy-start.27 = (bf16[256,512]{1,0:T(8,128)(2,1)}, bf16[256,512]{1,0:T(8,128)(2,1)S(1)}, u32[]{:S(2)}) copy-start(bf16[256,512]{1,0:T(8,128)(2,1)S(1)} %collective-permute-done.10.refs_7_) | copy-start | bytes 786436
  58.2 1.1 %copy-start.28 = (bf16[256,512]{1,0:T(8,128)(2,1)}, bf16[256,512]{1,0:T(8,128)(2,1)S(1)}, u32[]{:S(2)}) copy-start(bf16[256,512]{1,0:T(8,128)(2,1)S(1)} %collective-permute-done.8.refs_4_) | copy-start | bytes 786436
  58.2 1.1 %copy-start.29 = (bf16[256,512]{1,0:T(8,128)(2,1)}, bf16[256,512]{1,0:T(8,128)(2,1)S(1)}, u32[]{:S(2)}) copy-start(bf16[256,512]{1,0:T(8,128)(2,1)S(1)} %collective-permute-done.7.refs_3_) | copy-start | bytes 786436
  59.3 0.7 copy-start.30
  60.0 11.7 %copy-start.1 = (bf16[8,128,512]{2,1,0:T(8,128)(2,1)}, bf16[8,128,512]{2,1,0:T(8,128)(2,1)S(1)}, u32[]{:S(2)}) copy-start(bf16[8,128,512]{2,1,0:T(8,128)(2,1)S(1)} %all-to-all-done.1.blocks) | copy-start | bytes 3145732
  60.0 18.8 %all-to-all-start.2 = ((bf16[8,64,512]{2,1,0:T(8,128)(2,1)}), bf16[8,64,512]{2,1,0:T(8,128)(2,1)}, u32[]{:S(2)}, u32[]{:S(2)}) async-start(bf16[8,64,512]{2,1,0:T(8,128)(2,1)} %copy-done.10), calls=%async_computation.2 | async-start | bytes 1048576 | tf_op jit(solution)/shard_map/all_to_all | solution.py:270
  65.8 7.3 %copy-start.4 = (bf16[8,80,512]{2,1,0:T(8,128)(2,1)S(1)}, bf16[8,80,512]{2,1,0:T(8,128)(2,1)}, u32[]{:S(2)}) copy-start(bf16[8,80,512]{2,1,0:T(8,128)(2,1)} %copy-done.3) | copy-start | bytes 1966084
  65.8 7.3 %copy-start.15 = (bf16[512,64]{1,0:T(8,128)(2,1)S(1)}, bf16[512,64]{1,0:T(8,128)(2,1)}, u32[]{:S(2)}) copy-start(bf16[512,64]{1,0:T(8,128)(2,1)} %copy-done.14) | copy-start | bytes 196612
  65.8 16.6 %collective-permute-start.14 = (bf16[256,512]{1,0:T(8,128)(2,1)}, bf16[256,512]{1,0:T(8,128)(2,1)}, u32[]{:S(2)}, u32[]{:S(2)}) collective-permute-start(bf16[256,512]{1,0:T(8,128)(2,1)} %copy-done.25), channel_id=1, source_target_pairs={{0,16},{1,17},{2,18},{3,19},{4,20},{5,21},{6,22},{7,23},{8,24},{9,... | collective-permute-start | bytes 786440 | tf_op jit(solution)/shard_map/ppermute | solution.py:262
  67.4 15.1 %collective-permute-start.9 = (bf16[256,512]{1,0:T(8,128)(2,1)}, bf16[256,512]{1,0:T(8,128)(2,1)}, u32[]{:S(2)}, u32[]{:S(2)}) collective-permute-start(bf16[256,512]{1,0:T(8,128)(2,1)} %copy-done.28), channel_id=1, source_target_pairs={{0,16},{1,17},{2,18},{3,19},{4,20},{5,21},{6,22},{7,23},{8,24},{9,... | collective-permute-start | bytes 786440 | tf_op jit(solution)/shard_map/ppermute | solution.py:262
  67.9 15.6 %collective-permute-start.16 = (bf16[256,512]{1,0:T(8,128)(2,1)}, bf16[256,512]{1,0:T(8,128)(2,1)}, u32[]{:S(2)}, u32[]{:S(2)}) collective-permute-start(bf16[256,512]{1,0:T(8,128)(2,1)} %copy-done.30), channel_id=1, source_target_pairs={{0,16},{1,17},{2,18},{3,19},{4,20},{5,21},{6,22},{7,23},{8,24},{9,... | collective-permute-start | bytes 786440 | tf_op jit(solution)/shard_map/ppermute | solution.py:262
  71.7 1.4 %collective-permute-start.5 = (f32[256,64]{1,0:T(8,128)S(1)}, f32[256,64]{1,0:T(8,128)S(1)}, u32[]{:S(2)}, u32[]{:S(2)}) collective-permute-start(f32[256,64]{1,0:T(8,128)S(1)} %shard_map.105.low), channel_id=1, source_target_pairs={{0,1},{1,0},{2,3},{3,2},{4,5},{5,4},{6,7},{7,6},{8,9},{9,8},{10,11... | collective-permute-start | bytes 196616 | tf_op jit(solution)/shard_map/ppermute | solution.py:262
  74.7 0.8 copy-start.5
  78.9 20.3 %all-to-all-start.3 = ((bf16[8,80,512]{2,1,0:T(8,128)(2,1)}), bf16[8,80,512]{2,1,0:T(8,128)(2,1)S(1)}, u32[]{:S(2)}, u32[]{:S(2)}) async-start(bf16[8,80,512]{2,1,0:T(8,128)(2,1)} %copy-done.5), calls=%async_computation.3 | async-start | bytes 1310720 | tf_op jit(solution)/shard_map/all_to_all | solution.py:270
  82.4 12.5 %copy-start.18 = (s32[3]{0:T(128)S(1)}, s32[3]{0:T(128)}, u32[]{:S(2)}) copy-start(s32[3]{0:T(128)} %copy-done.17) | copy-start | bytes 40
  91.7 3.2 %collective-permute-start.18 = (bf16[128,4096]{1,0:T(8,128)(2,1)}, bf16[128,4096]{1,0:T(8,128)(2,1)S(1)}, u32[]{:S(2)}, u32[]{:S(2)}) collective-permute-start(bf16[128,4096]{1,0:T(8,128)(2,1)} %get-tuple-element.35), channel_id=1, source_target_pairs={{0,1},{1,0},{2,3},{3,2},{4,5},{5,4},{6,7},{7,6},{8,9},{9,8},{10,11... | collective-permute-start | bytes 3145736 | tf_op jit(solution)/shard_map/ppermute | solution.py:262
  91.7 3.2 %collective-permute-start.17 = (f32[128,512]{1,0:T(8,128)}, f32[128,512]{1,0:T(8,128)S(1)}, u32[]{:S(2)}, u32[]{:S(2)}) collective-permute-start(f32[128,512]{1,0:T(8,128)} %get-tuple-element.33), channel_id=1, source_target_pairs={{0,1},{1,0},{2,3},{3,2},{4,5},{5,4},{6,7},{7,6},{8,9},{9,8},{10,11... | collective-permute-start | bytes 786440 | tf_op jit(solution)/shard_map/ppermute | solution.py:262
  94.9 1.2 %copy-start.7 = (bf16[128,4096]{1,0:T(8,128)(2,1)S(1)}, bf16[128,4096]{1,0:T(8,128)(2,1)}, u32[]{:S(2)}) copy-start(bf16[128,4096]{1,0:T(8,128)(2,1)} %get-tuple-element.34.grad_mine) | copy-start | bytes 3145732
  96.1 0.9 copy-start.11

commit v2 on v1

--- a/solution.py
+++ b/solution.py
@@ -13,6 +13,7 @@
 BF16 = jnp.bfloat16
 VMEM = pl.BlockSpec(memory_space=pltpu.VMEM)
 SMEM = pl.BlockSpec(memory_space=pltpu.SMEM)
+HBM = pl.BlockSpec(memory_space=pltpu.HBM)
 
 
 def dot(a, b, ca, cb):
@@ -174,22 +175,28 @@
         low_own = dot(back_own[...], blocks[chip, 0:rank, inner], 1, 0).astype(BF16)
         low_sib = dot(back_sib[...], blocks[chip, rank : 2 * rank, inner], 1, 0).astype(BF16)
         to = pl.ds(pl.multiple_of(chip * width + shift, 128), count)
-        grad_own[:, to] = (grad[:rows] + low_own.astype(F32)).astype(BF16)
+        grad_own[:, pl.ds(start, count)] = (grad[:rows] + low_own.astype(F32)).astype(BF16)
         grad_sib[:, to] = (grad[rows:] + low_sib.astype(F32)).astype(BF16)
     for_own[...] = total[:rows]
     for_sib[...] = total[rows:]
 
 
-def join_kernel(chips, meta, mine, other, out_low, grad_mine, grad_other, result, grad_in):
-    c = meta[1]
+def join_kernel(chips, meta, mine, other, out_low, grad_other, grad_mine, result, grad_in, sems):
+    width = grad_other.shape[1] // chips
+    copies = []
+    for chip in range(chips):
+        to = pl.ds(pl.multiple_of((2 * chip + 1 - meta[1]) * width, width), width)
+        copies.append(
+            pltpu.make_async_copy(
+                grad_other.at[:, width * chip : width * (chip + 1)],
+                grad_in.at[:, to],
+                sems.at[chip],
+            )
+        )
+        copies[chip].start()
     result[...] = (mine[...] + other[...] + out_low[...]).astype(BF16)
-    width = grad_mine.shape[1] // chips
-    for chip in range(chips):
-        cols = slice(width * chip, width * (chip + 1))
-        own = pl.multiple_of((2 * chip + c) * width, width)
-        sib = pl.multiple_of((2 * chip + 1 - c) * width, width)
-        grad_in[:, pl.ds(own, width)] = grad_mine[:, cols]
-        grad_in[:, pl.ds(sib, width)] = grad_other[:, cols]
+    for copy in copies:
+        copy.wait()
 
 
 def back_kernel(meta, ids, first, second, down_out, up_out):
@@ -293,7 +300,7 @@
 
     (packed,) = call(pack_kernel, [shape((chips, 2 * rank, width))], (meta, ids), (adapter_down,))
     weights, plan, first, early = gather_weight(
-        base_weight, groups, size, send, (packed, up_parts)
+        base_weight, groups, size, send, (up_packed,)
     )
     blocks = exchange(after(packed, up_parts, tok_sib, og_sib, *first))
     first_back = exchange(after(grads_own, blocks, *early))
@@ -318,19 +325,23 @@
 
     for_own, for_sib, grad_own, grad_sib = call(
         functools.partial(base_kernel, plan),
-        [shape((rows, out_width), F32)] * 2 + [shape((rows, model_width // 2))] * 2,
+        [shape((rows, out_width), F32)] * 2
+        + [shape((rows, model_width)), shape((rows, model_width // 2))],
         (meta,),
         (tokens, tok_sib, out_grad, og_sib, after(back_own, out_low), back_sib, blocks, *weights),
         flops=4 * rows * model_width * out_width,
         room=60,
     )
     for_other, grad_other = sibling(for_sib), sibling(grad_sib)
-    result, grad_in = call(
+    result, grad_in = pl.pallas_call(
         functools.partial(join_kernel, chips),
-        [shape((rows, out_width)), shape((rows, model_width))],
-        (meta,),
-        (for_own, for_other, out_low, grad_own, grad_other),
-    )
+        out_shape=[shape((rows, out_width)), shape((rows, model_width))],
+        in_specs=[SMEM] + [VMEM] * 3 + [HBM] * 2,
+        out_specs=[VMEM, HBM],
+        scratch_shapes=[pltpu.SemaphoreType.DMA((chips,))],
+        input_output_aliases={5: 1},
+        compiler_params=pltpu.CompilerParams(vmem_limit_bytes=30 * 1024 * 1024),
+    )(meta, for_own, for_other, out_low, grad_other, grad_own)
     down_grad, up_grad = call(
         back_kernel,
         [shape(adapter_down.shape), shape(adapter_up.shape)],

time: 102 us -> 102 us (level)
  local copies, waits for them, and re-layouts: 12.2 us -> 11 us
    pallas_call x0 -> x1, Pallas kernels: none -> 2.22 us  [body(): pl.pallas_call(functools.partial(join_kernel, chips), out_shape=[shape((r...]
    pallas_call x8 -> x7, Pallas kernels: 20 us -> 18.2 us  [call(): pl.pallas_call(kernel, out_shape=outs, in_specs=[SMEM] * len(scalars) + [...]
    unnamed x62 -> x60, local copies, waits for them, and re-layouts: 11.2 us -> 10 us
  transfers between devices with their start and end apart: 23 -> 23, of which waited for: 7 -> 8; matrix products, arithmetic and copies ran while one was open for 1% -> 1% of each run, Pallas kernels for 19% -> 20%
where the time goes in v2:
time: 102 us; the launch traced here: 101 us
  starting transfers between devices  37.9 us (37%)
  waiting for transfers between devices  29.4 us (29%)
  Pallas kernels  22 us (22%)
  local copies, waits for them, and re-layouts  11 us (11%)
    ppermute x19, waiting for transfers between devices, send(): return lax.ppermute(x, AXES, pairs(groups, size, to))  22 us
    ppermute x19, starting transfers between devices, send(): return lax.ppermute(x, AXES, pairs(groups, size, to))  19.7 us
    pallas_call x7, Pallas kernels, call(): pl.pallas_call(kernel, out_shape=outs, in_specs=[SMEM] * len(scalars) + [...  18.2 us
    all_to_all x3, starting transfers between devices, exchange(): lax.all_to_all(blocks, 'dp', split_axis=0, concat_axis=0, tiled=True, axi...  14.7 us
    unnamed x60, local copies, waits for them, and re-layouts  10 us
    all_to_all x3, waiting for transfers between devices, exchange(): lax.all_to_all(blocks, 'dp', split_axis=0, concat_axis=0, tiled=True, axi...  4.05 us
    all_to_all x1, starting transfers between devices, body(): lax.all_to_all(up_packed, 'dp', split_axis=0, concat_axis=0, tiled=True)  3.52 us
    all_to_all x1, waiting for transfers between devices, body(): lax.all_to_all(up_packed, 'dp', split_axis=0, concat_axis=0, tiled=True)  3.29 us
  transfers between devices with their start and end apart: 23, of which 8 were waited for; matrix products, arithmetic and copies ran while one was open for 1% of the time, Pallas kernels for 20%

profile of v2, /device:TPU:0, one launch (start us, length us, event | category | flops | bytes accessed | tf_op | source)
XLA Modules:
  0.0 101.3 jit_solution(8880035906939705235)
XLA Ops:
  0.6 0.5 collective-permute-start
  1.1 1.0 constant_dynamic-slice_fusion
  2.1 2.6 %collective-permute-start.2 = (bf16[512,512]{1,0:T(8,128)(2,1)}, bf16[512,512]{1,0:T(8,128)(2,1)S(1)}, u32[]{:S(2)}, u32[]{:S(2)}) collective-permute-start(bf16[512,512]{1,0:T(8,128)(2,1)} %refs_0_.1), channel_id=1, source_target_pairs={{0,2},{1,3},{2,0},{3,1},{4,6},{5,7},{6,4},{7,5},{8,10},{9,11},{10,... | collective-permute-start | bytes 1572872 | tf_op jit(solution)/shard_map/ppermute | solution.py:269
  4.7 3.6 %collective-permute-start.4 = (bf16[256,512]{1,0:T(8,128)(2,1)S(1)}, bf16[256,512]{1,0:T(8,128)(2,1)}, u32[]{:S(2)}, u32[]{:S(2)}) collective-permute-start(bf16[256,512]{1,0:T(8,128)(2,1)S(1)} %constant_dynamic-slice_fusion), channel_id=1, source_target_pairs={{0,12},{1,13},{2,14},{3,15},{4,8},{5,9},{6,10},{7,11},{8,4},{9,5},... | collective-permute-start | bytes 786440 | tf_op jit(solution)/shard_map/ppermute | solution.py:269
  8.3 0.0 collective-permute-start.3
  8.3 0.0 collective-permute-start.1
  8.3 0.8 copy-done.15
  9.2 0.7 copy-done.18
  9.8 1.6 %shard_map.102 = bf16[16,16,128]{2,1,0:T(8,128)(2,1)} custom-call(s32[16]{0:T(128)S(1)} %bitcast.4, bf16[16,2048]{1,0:T(8,128)(2,1)S(1)} %copy-done.15), custom_call_target="tpu_custom_call" | custom-call | bytes 131072 | tf_op jit(solution)/shard_map/pallas_call | solution.py:26
  11.4 3.5 %all-to-all-start = ((bf16[16,16,128]{2,1,0:T(8,128)(2,1)}), bf16[16,16,128]{2,1,0:T(8,128)(2,1)S(1)}, u32[]{:S(2)}, u32[]{:S(2)}) async-start(bf16[16,16,128]{2,1,0:T(8,128)(2,1)} %shard_map.102), calls=%async_computation | async-start | bytes 131072 | tf_op jit(solution)/shard_map/all_to_all | solution.py:285
  15.0 0.1 pad_add_fusion.meta
  15.0 1.2 %copy-done.7 = bf16[16,64,512]{2,1,0:T(8,128)(2,1)S(1)} copy-done((bf16[16,64,512]{2,1,0:T(8,128)(2,1)S(1)}, bf16[16,64,512]{2,1,0:T(8,128)(2,1)}, u32[]{:S(2)}) %copy-start.7) | copy-done | bytes 1048600
  16.3 0.7 copy-done.19
  16.9 0.0 copy-start
  16.9 0.6 shard_map.104
  17.6 0.0 copy-start.2
  17.6 1.0 copy-done.2
  18.5 3.3 %all-to-all-done.packed = bf16[16,16,128]{2,1,0:T(8,128)(2,1)S(1)} async-done(((bf16[16,16,128]{2,1,0:T(8,128)(2,1)}), bf16[16,16,128]{2,1,0:T(8,128)(2,1)S(1)}, u32[]{:S(2)}, u32[]{:S(2)}) %all-to-all-start) | async-done | bytes 65568 | tf_op jit(solution)/shard_map/all_to_all | solution.py:285
  21.8 0.0 collective-permute-done.1.og_sib
  21.8 0.0 collective-permute-done.4.refs_6_
  21.8 0.0 collective-permute-done.3.refs_2_
  21.9 0.0 collective-permute-done.2.refs_1_
  21.9 0.7 copy-done.23
  22.6 0.2 copy-done.22
  22.8 5.3 %all-to-all-start.1 = ((bf16[8,128,512]{2,1,0:T(8,128)(2,1)}), bf16[8,128,512]{2,1,0:T(8,128)(2,1)S(1)}, u32[]{:S(2)}, u32[]{:S(2)}) async-start(bf16[8,128,512]{2,1,0:T(8,128)(2,1)} %copy-done.2), calls=%async_computation.1 | async-start | bytes 2097152 | tf_op jit(solution)/shard_map/all_to_all | solution.py:277
  28.1 2.0 %collective-permute-start.13 = (bf16[256,512]{1,0:T(8,128)(2,1)}, bf16[256,512]{1,0:T(8,128)(2,1)S(1)}, u32[]{:S(2)}, u32[]{:S(2)}) collective-permute-start(bf16[256,512]{1,0:T(8,128)(2,1)} %collective-permute-done.4.refs_6_), channel_id=1, source_target_pairs={{0,4},{1,5},{2,6},{3,7},{4,0},{5,1},{6,2},{7,3},{8,12},{9,13},{10,... | collective-permute-start | bytes 786440 | tf_op jit(solution)/shard_map/ppermute | solution.py:269
  30.1 1.5 %collective-permute-start.11 = (bf16[256,512]{1,0:T(8,128)(2,1)}, bf16[256,512]{1,0:T(8,128)(2,1)S(1)}, u32[]{:S(2)}, u32[]{:S(2)}) collective-permute-start(bf16[256,512]{1,0:T(8,128)(2,1)} %collective-permute-done.4.refs_6_), channel_id=1, source_target_pairs={{0,2},{1,3},{2,0},{3,1},{4,6},{5,7},{6,4},{7,5},{8,10},{9,11},{10,... | collective-permute-start | bytes 786440 | tf_op jit(solution)/shard_map/ppermute | solution.py:269
  31.6 1.1 %shard_map.103 = (bf16[512,64]{1,0:T(8,128)(2,1)S(1)}, bf16[128,64]{1,0:T(8,128)(2,1)S(1)}) custom-call(s32[3]{0:T(128)S(1)} %pad_add_fusion.meta, s32[16]{0:T(128)S(1)} %bitcast.6, s32[16]{0:T(128)S(1)} %copy-done.21, bf16[128,512]{1,0:T(8,128)(2,1)S(1)} %copy-done.6, bf16[16,16,128]{2,1,0:T(8,128)(2,1)S(1)} %all-to-all-done.packed), custom_call_target="tpu_custom_call" | custom-call | bytes 278528 | tf_op jit(solution)/shard_map/pallas_call | solution.py:26
  32.7 0.6 copy-done.13
  33.4 1.5 %collective-permute-start.10 = (bf16[256,512]{1,0:T(8,128)(2,1)}, bf16[256,512]{1,0:T(8,128)(2,1)S(1)}, u32[]{:S(2)}, u32[]{:S(2)}) collective-permute-start(bf16[256,512]{1,0:T(8,128)(2,1)} %collective-permute-done.4.refs_6_), channel_id=1, source_target_pairs={{0,16},{1,17},{2,18},{3,19},{4,20},{5,21},{6,22},{7,23},{8,24},{9,... | collective-permute-start | bytes 786440 | tf_op jit(solution)/shard_map/ppermute | solution.py:269
  34.8 0.6 collective-permute-start.8
  35.4 0.6 collective-permute-start.7
  36.1 15.7 %collective-permute-done.13.refs_10_ = bf16[256,512]{1,0:T(8,128)(2,1)S(1)} collective-permute-done((bf16[256,512]{1,0:T(8,128)(2,1)}, bf16[256,512]{1,0:T(8,128)(2,1)S(1)}, u32[]{:S(2)}, u32[]{:S(2)}) %collective-permute-start.13) | collective-permute-done | bytes 262176 | tf_op jit(solution)/shard_map/ppermute | solution.py:269
  51.8 1.1 %collective-permute-start.15 = (bf16[256,512]{1,0:T(8,128)(2,1)S(1)}, bf16[256,512]{1,0:T(8,128)(2,1)S(1)}, u32[]{:S(2)}, u32[]{:S(2)}) collective-permute-start(bf16[256,512]{1,0:T(8,128)(2,1)S(1)} %collective-permute-done.13.refs_10_), channel_id=1, source_target_pairs={{0,2},{1,3},{2,0},{3,1},{4,6},{5,7},{6,4},{7,5},{8,10},{9,11},{10,... | collective-permute-start | bytes 786440 | tf_op jit(solution)/shard_map/ppermute | solution.py:269
  52.9 1.5 %collective-permute-start.12 = (bf16[256,512]{1,0:T(8,128)(2,1)S(1)}, bf16[256,512]{1,0:T(8,128)(2,1)}, u32[]{:S(2)}, u32[]{:S(2)}) collective-permute-start(bf16[256,512]{1,0:T(8,128)(2,1)S(1)} %collective-permute-done.11.refs_8_), channel_id=1, source_target_pairs={{0,16},{1,17},{2,18},{3,19},{4,20},{5,21},{6,22},{7,23},{8,24},{9,... | collective-permute-start | bytes 786440 | tf_op jit(solution)/shard_map/ppermute | solution.py:269
  54.4 2.1 %shard_map.106 = (bf16[8,64,512]{2,1,0:T(8,128)(2,1)S(1)}, bf16[8,80,512]{2,1,0:T(8,128)(2,1)S(1)}) custom-call(s32[3]{0:T(128)S(1)} %pad_add_fusion.meta, bf16[128,8192]{1,0:T(8,128)(2,1)S(1)} %copy-done, bf16[128,8192]{1,0:T(8,128)(2,1)} %collective-permute-done.tok_sib, bf16[128,64]{1,0:T(8,128)(2,1)S(1)} %get-tuple-element.30.back_own, ...), custom_call_target="tpu_custom_call" | custom-call | flops 134217728 | bytes 5406720 | tf_op jit(solution)/shard_map/pallas_call | solution.py:26
  56.5 0.0 copy-start.3
  56.5 0.8 copy-done.3
  57.4 0.8 copy-done.9
  58.1 0.0 collective-permute-done.10.refs_7_
  58.2 0.0 collective-permute-done.7.refs_3_
  58.2 1.1 %collective-permute-done.15.refs_12_ = bf16[256,512]{1,0:T(8,128)(2,1)S(1)} collective-permute-done((bf16[256,512]{1,0:T(8,128)(2,1)S(1)}, bf16[256,512]{1,0:T(8,128)(2,1)S(1)}, u32[]{:S(2)}, u32[]{:S(2)}) %collective-permute-start.15) | collective-permute-done | bytes 262176 | tf_op jit(solution)/shard_map/ppermute | solution.py:269
  59.3 0.7 copy-done.29
  60.0 0.0 collective-permute-done.12.refs_9_
  60.0 0.0 all-to-all-done.1.blocks
  60.0 5.8 %all-to-all-start.2 = ((bf16[8,64,512]{2,1,0:T(8,128)(2,1)}), bf16[8,64,512]{2,1,0:T(8,128)(2,1)}, u32[]{:S(2)}, u32[]{:S(2)}) async-start(bf16[8,64,512]{2,1,0:T(8,128)(2,1)} %copy-done.9), calls=%async_computation.2 | async-start | bytes 1048576 | tf_op jit(solution)/shard_map/all_to_all | solution.py:277
  65.8 1.6 %collective-permute-start.14 = (bf16[256,512]{1,0:T(8,128)(2,1)}, bf16[256,512]{1,0:T(8,128)(2,1)}, u32[]{:S(2)}, u32[]{:S(2)}) collective-permute-start(bf16[256,512]{1,0:T(8,128)(2,1)} %copy-done.24), channel_id=1, source_target_pairs={{0,16},{1,17},{2,18},{3,19},{4,20},{5,21},{6,22},{7,23},{8,24},{9,... | collective-permute-start | bytes 786440 | tf_op jit(solution)/shard_map/ppermute | solution.py:269
  67.4 0.5 collective-permute-start.9
  67.9 1.5 %collective-permute-start.16 = (bf16[256,512]{1,0:T(8,128)(2,1)}, bf16[256,512]{1,0:T(8,128)(2,1)}, u32[]{:S(2)}, u32[]{:S(2)}) collective-permute-start(bf16[256,512]{1,0:T(8,128)(2,1)} %copy-done.29), channel_id=1, source_target_pairs={{0,16},{1,17},{2,18},{3,19},{4,20},{5,21},{6,22},{7,23},{8,24},{9,... | collective-permute-start | bytes 786440 | tf_op jit(solution)/shard_map/ppermute | solution.py:269
  69.4 2.3 %shard_map.105.low = f32[256,64]{1,0:T(8,128)S(1)} custom-call(s32[3]{0:T(128)S(1)} %pad_add_fusion.meta, bf16[128,8192]{1,0:T(8,128)(2,1)S(1)} %copy-done, bf16[128,8192]{1,0:T(8,128)(2,1)} %collective-permute-done.tok_sib, bf16[8,128,512]{2,1,0:T(8,128)(2,1)S(1)} %all-to-all-done.1.blocks), custom_call_target="tpu_custom_call" | custom-call | flops 134217728 | bytes 5308416 | tf_op jit(solution)/shard_map/pallas_call | solution.py:26
  71.7 0.1 collective-permute-start.5
  71.8 1.3 %collective-permute-done.5.other = f32[256,64]{1,0:T(8,128)S(1)} collective-permute-done((f32[256,64]{1,0:T(8,128)S(1)}, f32[256,64]{1,0:T(8,128)S(1)}, u32[]{:S(2)}, u32[]{:S(2)}) %collective-permute-start.5) | collective-permute-done | bytes 65568 | tf_op jit(solution)/shard_map/ppermute | solution.py:269
  73.1 1.6 %shard_map.107 = (f32[128,512]{1,0:T(8,128)S(1)}, bf16[8,80,512]{2,1,0:T(8,128)(2,1)S(1)}) custom-call(s32[3]{0:T(128)S(1)} %pad_add_fusion.meta, s32[16]{0:T(128)S(1)} %bitcast.7, s32[16]{0:T(128)S(1)} %copy-done.21, f32[256,64]{1,0:T(8,128)S(1)} %shard_map.105.low, f32[256,64]{1,0:T(8,128)S(1)} %collective-permute-done.5.other, ...), custom_call_target="tpu_custom_call", output_to_operand_aliasing={{1}: (8, {})} | custom-call | tf_op jit(solution)/shard_map/pallas_call | solution.py:315
  74.7 0.8 copy-done.5
  75.6 3.3 %all-to-all-done.2.first = bf16[8,64,512]{2,1,0:T(8,128)(2,1)} async-done(((bf16[8,64,512]{2,1,0:T(8,128)(2,1)}), bf16[8,64,512]{2,1,0:T(8,128)(2,1)}, u32[]{:S(2)}, u32[]{:S(2)}) %all-to-all-start.2) | async-done | bytes 524320 | tf_op jit(solution)/shard_map/all_to_all | solution.py:277
  78.9 3.5 %all-to-all-start.3 = ((bf16[8,80,512]{2,1,0:T(8,128)(2,1)}), bf16[8,80,512]{2,1,0:T(8,128)(2,1)S(1)}, u32[]{:S(2)}, u32[]{:S(2)}) async-start(bf16[8,80,512]{2,1,0:T(8,128)(2,1)} %copy-done.5), calls=%async_computation.3 | async-start | bytes 1310720 | tf_op jit(solution)/shard_map/all_to_all | solution.py:277
  82.5 1.1 %collective-permute-done.16.refs_13_ = bf16[256,512]{1,0:T(8,128)(2,1)} collective-permute-done((bf16[256,512]{1,0:T(8,128)(2,1)}, bf16[256,512]{1,0:T(8,128)(2,1)}, u32[]{:S(2)}, u32[]{:S(2)}) %collective-permute-start.16) | collective-permute-done | bytes 262176 | tf_op jit(solution)/shard_map/ppermute | solution.py:269
  83.6 8.4 %shard_map.108 = (f32[128,512]{1,0:T(8,128)}, f32[128,512]{1,0:T(8,128)}, bf16[128,8192]{1,0:T(8,128)(2,1)}, bf16[128,4096]{1,0:T(8,128)(2,1)}) custom-call(s32[3]{0:T(128)} %copy-done.16, bf16[128,8192]{1,0:T(8,128)(2,1)} %tok_own.5, bf16[128,8192]{1,0:T(8,128)(2,1)} %collective-permute-done.tok_sib, bf16[128,512]{1,0:T(8,128)(2,1)} %og_own.3, ...), custom_call_target="tpu_custom_call" | custom-call | flops 2147483648 | bytes 13402112 | tf_op jit(solution)/shard_map/pallas_call | solution.py:26
  92.0 0.5 collective-permute-start.17
  92.5 2.7 %collective-permute-done.17.other = f32[128,512]{1,0:T(8,128)S(1)} collective-permute-done((f32[128,512]{1,0:T(8,128)}, f32[128,512]{1,0:T(8,128)S(1)}, u32[]{:S(2)}, u32[]{:S(2)}) %collective-permute-start.17) | collective-permute-done | bytes 262176 | tf_op jit(solution)/shard_map/ppermute | solution.py:269
  95.2 0.9 copy-done.10
  96.2 2.2 %shard_map.109 = (bf16[128,512]{1,0:T(8,128)(2,1)}, bf16[128,8192]{1,0:T(8,128)(2,1)}) custom-call(s32[3]{0:T(128)S(1)} %copy-done.17, f32[128,512]{1,0:T(8,128)S(1)} %copy-done.10, f32[128,512]{1,0:T(8,128)S(1)} %collective-permute-done.17.other, f32[128,512]{1,0:T(8,128)S(1)} %get-tuple-element.29.out_low, ...), custom_call_target="tpu_custom_call", output_to_operand_aliasing={{1}: (5, {})} | custom-call | tf_op jit(solution)/shard_map/pallas_call | solution.py:336
  98.4 0.7 all-to-all-done.3.second
  99.1 2.1 %shard_map.110 = (bf16[16,64,512]{2,1,0:T(8,128)(2,1)}, bf16[16,2048]{1,0:T(8,128)(2,1)}) custom-call(s32[3]{0:T(128)S(1)} %copy-done.17, s32[16]{0:T(128)S(1)} %bitcast.8, bf16[8,64,512]{2,1,0:T(8,128)(2,1)} %all-to-all-done.2.first, bf16[8,80,512]{2,1,0:T(8,128)(2,1)S(1)} %all-to-all-done.3.second), custom_call_target="tpu_custom_call" | custom-call | bytes 2293760 | tf_op jit(solution)/shard_map/pallas_call | solution.py:26
  (53 shorter events, 0.1 us)
Async XLA Ops:
  0.6 21.3 %collective-permute-start = (bf16[128,8192]{1,0:T(8,128)(2,1)}, bf16[128,8192]{1,0:T(8,128)(2,1)}, u32[]{:S(2)}, u32[]{:S(2)}) collective-permute-start(bf16[128,8192]{1,0:T(8,128)(2,1)} %tok_own.5), channel_id=1, source_target_pairs={{0,1},{1,0},{2,3},{3,2},{4,5},{5,4},{6,7},{7,6},{8,9},{9,8},{10,11... | collective-permute-start | bytes 6291464 | tf_op jit(solution)/shard_map/ppermute | solution.py:269
  2.1 19.8 %collective-permute-start.2 = (bf16[512,512]{1,0:T(8,128)(2,1)}, bf16[512,512]{1,0:T(8,128)(2,1)S(1)}, u32[]{:S(2)}, u32[]{:S(2)}) collective-permute-start(bf16[512,512]{1,0:T(8,128)(2,1)} %refs_0_.1), channel_id=1, source_target_pairs={{0,2},{1,3},{2,0},{3,1},{4,6},{5,7},{6,4},{7,5},{8,10},{9,11},{10,... | collective-permute-start | bytes 1572872 | tf_op jit(solution)/shard_map/ppermute | solution.py:269
  4.7 17.1 %collective-permute-start.4 = (bf16[256,512]{1,0:T(8,128)(2,1)S(1)}, bf16[256,512]{1,0:T(8,128)(2,1)}, u32[]{:S(2)}, u32[]{:S(2)}) collective-permute-start(bf16[256,512]{1,0:T(8,128)(2,1)S(1)} %constant_dynamic-slice_fusion), channel_id=1, source_target_pairs={{0,12},{1,13},{2,14},{3,15},{4,8},{5,9},{6,10},{7,11},{8,4},{9,5},... | collective-permute-start | bytes 786440 | tf_op jit(solution)/shard_map/ppermute | solution.py:269
  8.3 13.5 %collective-permute-start.3 = (bf16[256,512]{1,0:T(8,128)(2,1)S(1)}, bf16[256,512]{1,0:T(8,128)(2,1)S(1)}, u32[]{:S(2)}, u32[]{:S(2)}) collective-permute-start(bf16[256,512]{1,0:T(8,128)(2,1)S(1)} %constant_dynamic-slice_fusion), channel_id=1, source_target_pairs={{0,4},{1,5},{2,6},{3,7},{4,0},{5,1},{6,2},{7,3},{8,12},{9,13},{10,... | collective-permute-start | bytes 786440 | tf_op jit(solution)/shard_map/ppermute | solution.py:269
  8.3 13.5 %collective-permute-start.1 = (bf16[128,512]{1,0:T(8,128)(2,1)}, bf16[128,512]{1,0:T(8,128)(2,1)S(1)}, u32[]{:S(2)}, u32[]{:S(2)}) collective-permute-start(bf16[128,512]{1,0:T(8,128)(2,1)} %og_own.3), channel_id=1, source_target_pairs={{0,1},{1,0},{2,3},{3,2},{4,5},{5,4},{6,7},{7,6},{8,9},{9,8},{10,11... | collective-permute-start | bytes 393224 | tf_op jit(solution)/shard_map/ppermute | solution.py:269
  8.3 0.8 copy-start.15
  9.2 0.7 copy-start.18
  11.4 10.4 %all-to-all-start = ((bf16[16,16,128]{2,1,0:T(8,128)(2,1)}), bf16[16,16,128]{2,1,0:T(8,128)(2,1)S(1)}, u32[]{:S(2)}, u32[]{:S(2)}) async-start(bf16[16,16,128]{2,1,0:T(8,128)(2,1)} %shard_map.102), calls=%async_computation | async-start | bytes 131072 | tf_op jit(solution)/shard_map/all_to_all | solution.py:285
  15.0 1.2 %copy-start.7 = (bf16[16,64,512]{2,1,0:T(8,128)(2,1)S(1)}, bf16[16,64,512]{2,1,0:T(8,128)(2,1)}, u32[]{:S(2)}) copy-start(bf16[16,64,512]{2,1,0:T(8,128)(2,1)} %down.1) | copy-start | bytes 3145732
  16.3 0.7 copy-start.19
  16.9 56.2 %copy-start.16 = (s32[3]{0:T(128)}, s32[3]{0:T(128)S(1)}, u32[]{:S(2)}) copy-start(s32[3]{0:T(128)S(1)} %pad_add_fusion.meta) | copy-start | bytes 40
  16.9 14.7 %copy-start.6 = (bf16[128,512]{1,0:T(8,128)(2,1)S(1)}, bf16[128,512]{1,0:T(8,128)(2,1)}, u32[]{:S(2)}) copy-start(bf16[128,512]{1,0:T(8,128)(2,1)} %og_own.3) | copy-start | bytes 393220
  16.9 14.7 %copy-start.20 = (s32[16,1]{0,1:T(1,128)S(1)}, s32[16,1]{0,1:T(1,128)}, u32[]{:S(2)}) copy-start(s32[16,1]{0,1:T(1,128)} %param.13) | copy-start | bytes 196
  16.9 14.7 %copy-start.21 = (s32[16]{0:T(128)S(1)}, s32[16]{0:T(128)}, u32[]{:S(2)}) copy-start(s32[16]{0:T(128)} %ranks.3) | copy-start | bytes 196
  16.9 37.5 %copy-start = (bf16[128,8192]{1,0:T(8,128)(2,1)S(1)}, bf16[128,8192]{1,0:T(8,128)(2,1)}, u32[]{:S(2)}) copy-start(bf16[128,8192]{1,0:T(8,128)(2,1)} %tok_own.5) | copy-start | bytes 6291460
  17.6 1.0 copy-start.2
  21.8 51.3 %copy-start.8 = (bf16[128,512]{1,0:T(8,128)(2,1)}, bf16[128,512]{1,0:T(8,128)(2,1)S(1)}, u32[]{:S(2)}) copy-start(bf16[128,512]{1,0:T(8,128)(2,1)S(1)} %collective-permute-done.1.og_sib) | copy-start | bytes 393220
  21.9 0.7 copy-start.23
  21.9 0.9 copy-start.22
  22.8 37.2 %all-to-all-start.1 = ((bf16[8,128,512]{2,1,0:T(8,128)(2,1)}), bf16[8,128,512]{2,1,0:T(8,128)(2,1)S(1)}, u32[]{:S(2)}, u32[]{:S(2)}) async-start(bf16[8,128,512]{2,1,0:T(8,128)(2,1)} %copy-done.2), calls=%async_computation.1 | async-start | bytes 2097152 | tf_op jit(solution)/shard_map/all_to_all | solution.py:277
  28.1 23.7 %collective-permute-start.13 = (bf16[256,512]{1,0:T(8,128)(2,1)}, bf16[256,512]{1,0:T(8,128)(2,1)S(1)}, u32[]{:S(2)}, u32[]{:S(2)}) collective-permute-start(bf16[256,512]{1,0:T(8,128)(2,1)} %collective-permute-done.4.refs_6_), channel_id=1, source_target_pairs={{0,4},{1,5},{2,6},{3,7},{4,0},{5,1},{6,2},{7,3},{8,12},{9,13},{10,... | collective-permute-start | bytes 786440 | tf_op jit(solution)/shard_map/ppermute | solution.py:269
  30.1 22.8 %collective-permute-start.11 = (bf16[256,512]{1,0:T(8,128)(2,1)}, bf16[256,512]{1,0:T(8,128)(2,1)S(1)}, u32[]{:S(2)}, u32[]{:S(2)}) collective-permute-start(bf16[256,512]{1,0:T(8,128)(2,1)} %collective-permute-done.4.refs_6_), channel_id=1, source_target_pairs={{0,2},{1,3},{2,0},{3,1},{4,6},{5,7},{6,4},{7,5},{8,10},{9,11},{10,... | collective-permute-start | bytes 786440 | tf_op jit(solution)/shard_map/ppermute | solution.py:269
  32.7 0.6 copy-start.13
  33.3 23.1 %copy-start.11 = (bf16[128,64]{1,0:T(8,128)(2,1)}, bf16[128,64]{1,0:T(8,128)(2,1)S(1)}, u32[]{:S(2)}) copy-start(bf16[128,64]{1,0:T(8,128)(2,1)S(1)} %get-tuple-element.30.back_own) | copy-start | bytes 49156
  33.4 2.1 %collective-permute-start.6 = (bf16[128,64]{1,0:T(8,128)(2,1)S(1)}, bf16[128,64]{1,0:T(8,128)(2,1)S(1)}, u32[]{:S(2)}, u32[]{:S(2)}) collective-permute-start(bf16[128,64]{1,0:T(8,128)(2,1)S(1)} %get-tuple-element.30.back_own), channel_id=1, source_target_pairs={{0,1},{1,0},{2,3},{3,2},{4,5},{5,4},{6,7},{7,6},{8,9},{9,8},{10,11... | collective-permute-start | bytes 49160 | tf_op jit(solution)/shard_map/ppermute | solution.py:269
  33.4 24.8 %collective-permute-start.10 = (bf16[256,512]{1,0:T(8,128)(2,1)}, bf16[256,512]{1,0:T(8,128)(2,1)S(1)}, u32[]{:S(2)}, u32[]{:S(2)}) collective-permute-start(bf16[256,512]{1,0:T(8,128)(2,1)} %collective-permute-done.4.refs_6_), channel_id=1, source_target_pairs={{0,16},{1,17},{2,18},{3,19},{4,20},{5,21},{6,22},{7,23},{8,24},{9,... | collective-permute-start | bytes 786440 | tf_op jit(solution)/shard_map/ppermute | solution.py:269
  34.8 23.3 %collective-permute-start.8 = (bf16[256,512]{1,0:T(8,128)(2,1)}, bf16[256,512]{1,0:T(8,128)(2,1)S(1)}, u32[]{:S(2)}, u32[]{:S(2)}) collective-permute-start(bf16[256,512]{1,0:T(8,128)(2,1)} %copy-done.23), channel_id=1, source_target_pairs={{0,2},{1,3},{2,0},{3,1},{4,6},{5,7},{6,4},{7,5},{8,10},{9,11},{10,... | collective-permute-start | bytes 786440 | tf_op jit(solution)/shard_map/ppermute | solution.py:269
  35.4 21.1 %copy-start.12 = (bf16[128,64]{1,0:T(8,128)(2,1)}, bf16[128,64]{1,0:T(8,128)(2,1)S(1)}, u32[]{:S(2)}) copy-start(bf16[128,64]{1,0:T(8,128)(2,1)S(1)} %collective-permute-done.6.back_sib) | copy-start | bytes 49156
  35.4 22.8 %collective-permute-start.7 = (bf16[256,512]{1,0:T(8,128)(2,1)}, bf16[256,512]{1,0:T(8,128)(2,1)S(1)}, u32[]{:S(2)}, u32[]{:S(2)}) collective-permute-start(bf16[256,512]{1,0:T(8,128)(2,1)} %copy-done.23), channel_id=1, source_target_pairs={{0,16},{1,17},{2,18},{3,19},{4,20},{5,21},{6,22},{7,23},{8,24},{9,... | collective-permute-start | bytes 786440 | tf_op jit(solution)/shard_map/ppermute | solution.py:269
  51.8 4.7 %copy-start.24 = (bf16[256,512]{1,0:T(8,128)(2,1)}, bf16[256,512]{1,0:T(8,128)(2,1)S(1)}, u32[]{:S(2)}) copy-start(bf16[256,512]{1,0:T(8,128)(2,1)S(1)} %collective-permute-done.13.refs_10_) | copy-start | bytes 786436
  51.8 7.5 %collective-permute-start.15 = (bf16[256,512]{1,0:T(8,128)(2,1)S(1)}, bf16[256,512]{1,0:T(8,128)(2,1)S(1)}, u32[]{:S(2)}, u32[]{:S(2)}) collective-permute-start(bf16[256,512]{1,0:T(8,128)(2,1)S(1)} %collective-permute-done.13.refs_10_), channel_id=1, source_target_pairs={{0,2},{1,3},{2,0},{3,1},{4,6},{5,7},{6,4},{7,5},{8,10},{9,11},{10,... | collective-permute-start | bytes 786440 | tf_op jit(solution)/shard_map/ppermute | solution.py:269
  52.9 3.6 %copy-start.25 = (bf16[256,512]{1,0:T(8,128)(2,1)}, bf16[256,512]{1,0:T(8,128)(2,1)S(1)}, u32[]{:S(2)}) copy-start(bf16[256,512]{1,0:T(8,128)(2,1)S(1)} %collective-permute-done.11.refs_8_) | copy-start | bytes 786436
  52.9 7.1 %collective-permute-start.12 = (bf16[256,512]{1,0:T(8,128)(2,1)S(1)}, bf16[256,512]{1,0:T(8,128)(2,1)}, u32[]{:S(2)}, u32[]{:S(2)}) collective-permute-start(bf16[256,512]{1,0:T(8,128)(2,1)S(1)} %collective-permute-done.11.refs_8_), channel_id=1, source_target_pairs={{0,16},{1,17},{2,18},{3,19},{4,20},{5,21},{6,22},{7,23},{8,24},{9,... | collective-permute-start | bytes 786440 | tf_op jit(solution)/shard_map/ppermute | solution.py:269
  56.5 0.8 copy-start.3
  57.4 0.8 copy-start.9
  58.2 1.1 %copy-start.26 = (bf16[256,512]{1,0:T(8,128)(2,1)}, bf16[256,512]{1,0:T(8,128)(2,1)S(1)}, u32[]{:S(2)}) copy-start(bf16[256,512]{1,0:T(8,128)(2,1)S(1)} %collective-permute-done.10.refs_7_) | copy-start | bytes 786436
  58.2 1.1 %copy-start.27 = (bf16[256,512]{1,0:T(8,128)(2,1)}, bf16[256,512]{1,0:T(8,128)(2,1)S(1)}, u32[]{:S(2)}) copy-start(bf16[256,512]{1,0:T(8,128)(2,1)S(1)} %collective-permute-done.8.refs_4_) | copy-start | bytes 786436
  58.2 1.1 %copy-start.28 = (bf16[256,512]{1,0:T(8,128)(2,1)}, bf16[256,512]{1,0:T(8,128)(2,1)S(1)}, u32[]{:S(2)}) copy-start(bf16[256,512]{1,0:T(8,128)(2,1)S(1)} %collective-permute-done.7.refs_3_) | copy-start | bytes 786436
  59.3 0.7 copy-start.29
  60.0 11.7 %copy-start.1 = (bf16[8,128,512]{2,1,0:T(8,128)(2,1)}, bf16[8,128,512]{2,1,0:T(8,128)(2,1)S(1)}, u32[]{:S(2)}) copy-start(bf16[8,128,512]{2,1,0:T(8,128)(2,1)S(1)} %all-to-all-done.1.blocks) | copy-start | bytes 3145732
  60.0 18.9 %all-to-all-start.2 = ((bf16[8,64,512]{2,1,0:T(8,128)(2,1)}), bf16[8,64,512]{2,1,0:T(8,128)(2,1)}, u32[]{:S(2)}, u32[]{:S(2)}) async-start(bf16[8,64,512]{2,1,0:T(8,128)(2,1)} %copy-done.9), calls=%async_computation.2 | async-start | bytes 1048576 | tf_op jit(solution)/shard_map/all_to_all | solution.py:277
  65.8 7.3 %copy-start.4 = (bf16[8,80,512]{2,1,0:T(8,128)(2,1)S(1)}, bf16[8,80,512]{2,1,0:T(8,128)(2,1)}, u32[]{:S(2)}) copy-start(bf16[8,80,512]{2,1,0:T(8,128)(2,1)} %copy-done.3) | copy-start | bytes 1966084
  65.8 7.3 %copy-start.14 = (bf16[512,64]{1,0:T(8,128)(2,1)S(1)}, bf16[512,64]{1,0:T(8,128)(2,1)}, u32[]{:S(2)}) copy-start(bf16[512,64]{1,0:T(8,128)(2,1)} %copy-done.13) | copy-start | bytes 196612
  65.8 16.6 %collective-permute-start.14 = (bf16[256,512]{1,0:T(8,128)(2,1)}, bf16[256,512]{1,0:T(8,128)(2,1)}, u32[]{:S(2)}, u32[]{:S(2)}) collective-permute-start(bf16[256,512]{1,0:T(8,128)(2,1)} %copy-done.24), channel_id=1, source_target_pairs={{0,16},{1,17},{2,18},{3,19},{4,20},{5,21},{6,22},{7,23},{8,24},{9,... | collective-permute-start | bytes 786440 | tf_op jit(solution)/shard_map/ppermute | solution.py:269
  67.4 15.1 %collective-permute-start.9 = (bf16[256,512]{1,0:T(8,128)(2,1)}, bf16[256,512]{1,0:T(8,128)(2,1)}, u32[]{:S(2)}, u32[]{:S(2)}) collective-permute-start(bf16[256,512]{1,0:T(8,128)(2,1)} %copy-done.27), channel_id=1, source_target_pairs={{0,16},{1,17},{2,18},{3,19},{4,20},{5,21},{6,22},{7,23},{8,24},{9,... | collective-permute-start | bytes 786440 | tf_op jit(solution)/shard_map/ppermute | solution.py:269
  67.9 15.6 %collective-permute-start.16 = (bf16[256,512]{1,0:T(8,128)(2,1)}, bf16[256,512]{1,0:T(8,128)(2,1)}, u32[]{:S(2)}, u32[]{:S(2)}) collective-permute-start(bf16[256,512]{1,0:T(8,128)(2,1)} %copy-done.29), channel_id=1, source_target_pairs={{0,16},{1,17},{2,18},{3,19},{4,20},{5,21},{6,22},{7,23},{8,24},{9,... | collective-permute-start | bytes 786440 | tf_op jit(solution)/shard_map/ppermute | solution.py:269
  71.7 1.4 %collective-permute-start.5 = (f32[256,64]{1,0:T(8,128)S(1)}, f32[256,64]{1,0:T(8,128)S(1)}, u32[]{:S(2)}, u32[]{:S(2)}) collective-permute-start(f32[256,64]{1,0:T(8,128)S(1)} %shard_map.105.low), channel_id=1, source_target_pairs={{0,1},{1,0},{2,3},{3,2},{4,5},{5,4},{6,7},{7,6},{8,9},{9,8},{10,11... | collective-permute-start | bytes 196616 | tf_op jit(solution)/shard_map/ppermute | solution.py:269
  74.7 0.8 copy-start.5
  78.9 20.2 %all-to-all-start.3 = ((bf16[8,80,512]{2,1,0:T(8,128)(2,1)}), bf16[8,80,512]{2,1,0:T(8,128)(2,1)S(1)}, u32[]{:S(2)}, u32[]{:S(2)}) async-start(bf16[8,80,512]{2,1,0:T(8,128)(2,1)} %copy-done.5), calls=%async_computation.3 | async-start | bytes 1310720 | tf_op jit(solution)/shard_map/all_to_all | solution.py:277
  82.4 12.8 %copy-start.17 = (s32[3]{0:T(128)S(1)}, s32[3]{0:T(128)}, u32[]{:S(2)}) copy-start(s32[3]{0:T(128)} %copy-done.16) | copy-start | bytes 40
  92.0 3.2 %collective-permute-start.18 = (bf16[128,4096]{1,0:T(8,128)(2,1)}, bf16[128,4096]{1,0:T(8,128)(2,1)S(1)}, u32[]{:S(2)}, u32[]{:S(2)}) collective-permute-start(bf16[128,4096]{1,0:T(8,128)(2,1)} %get-tuple-element.34), channel_id=1, source_target_pairs={{0,1},{1,0},{2,3},{3,2},{4,5},{5,4},{6,7},{7,6},{8,9},{9,8},{10,11... | collective-permute-start | bytes 3145736 | tf_op jit(solution)/shard_map/ppermute | solution.py:269
  92.0 3.2 %collective-permute-start.17 = (f32[128,512]{1,0:T(8,128)}, f32[128,512]{1,0:T(8,128)S(1)}, u32[]{:S(2)}, u32[]{:S(2)}) collective-permute-start(f32[128,512]{1,0:T(8,128)} %get-tuple-element.33), channel_id=1, source_target_pairs={{0,1},{1,0},{2,3},{3,2},{4,5},{5,4},{6,7},{7,6},{8,9},{9,8},{10,11... | collective-permute-start | bytes 786440 | tf_op jit(solution)/shard_map/ppermute | solution.py:269
  95.2 1.0 copy-start.10

commit v3 on v2

--- a/solution.py
+++ b/solution.py
@@ -302,7 +302,7 @@
     weights, plan, first, early = gather_weight(
         base_weight, groups, size, send, (up_packed,)
     )
-    blocks = exchange(after(packed, up_parts, tok_sib, og_sib, *first))
+    blocks = exchange(after(packed, tok_sib, og_sib, *first))
     first_back = exchange(after(grads_own, blocks, *early))
     (low,) = call(
         low_kernel,

time: 102 us -> 101 us (level)
    all_to_all x1, waiting for transfers between devices: 3.29 us -> 0.4 us  [body(): lax.all_to_all(up_packed, 'dp', split_axis=0, concat_axis=0, tiled=True)]
    ppermute x19, waiting for transfers between devices: 22 us -> 24.9 us  [send(): return lax.ppermute(x, AXES, pairs(groups, size, to))]
  transfers between devices with their start and end apart: 23 -> 23, of which waited for: 8 -> 9; matrix products, arithmetic and copies ran while one was open for 1% -> 1% of each run, Pallas kernels for 20% -> 20%
where the time goes in v3:
time: 101 us; the launch traced here: 100 us
  starting transfers between devices  37.4 us (37%)
  waiting for transfers between devices  29.3 us (29%)
  Pallas kernels  22 us (22%)
  local copies, waits for them, and re-layouts  10.6 us (10%)
    ppermute x19, waiting for transfers between devices, send(): return lax.ppermute(x, AXES, pairs(groups, size, to))  24.9 us
    ppermute x19, starting transfers between devices, send(): return lax.ppermute(x, AXES, pairs(groups, size, to))  19.7 us
    pallas_call x7, Pallas kernels, call(): pl.pallas_call(kernel, out_shape=outs, in_specs=[SMEM] * len(scalars) + [...  18.2 us
    all_to_all x3, starting transfers between devices, exchange(): lax.all_to_all(blocks, 'dp', split_axis=0, concat_axis=0, tiled=True, axi...  14.2 us
    unnamed x60, local copies, waits for them, and re-layouts  9.62 us
    all_to_all x3, waiting for transfers between devices, exchange(): lax.all_to_all(blocks, 'dp', split_axis=0, concat_axis=0, tiled=True, axi...  4.06 us
    all_to_all x1, starting transfers between devices, body(): lax.all_to_all(up_packed, 'dp', split_axis=0, concat_axis=0, tiled=True)  3.52 us
    pallas_call x1, Pallas kernels, body(): pl.pallas_call(functools.partial(join_kernel, chips), out_shape=[shape((r...  2.22 us
  transfers between devices with their start and end apart: 23, of which 9 were waited for; matrix products, arithmetic and copies ran while one was open for 1% of the time, Pallas kernels for 20%

profile of v3, /device:TPU:0, one launch (start us, length us, event | category | flops | bytes accessed | tf_op | source)
XLA Modules:
  0.0 100.3 jit_solution(15309348756481633313)
XLA Ops:
  0.6 0.5 collective-permute-start
  1.1 1.0 constant_dynamic-slice_fusion
  2.1 2.6 %collective-permute-start.2 = (bf16[512,512]{1,0:T(8,128)(2,1)}, bf16[512,512]{1,0:T(8,128)(2,1)S(1)}, u32[]{:S(2)}, u32[]{:S(2)}) collective-permute-start(bf16[512,512]{1,0:T(8,128)(2,1)} %refs_0_.1), channel_id=1, source_target_pairs={{0,2},{1,3},{2,0},{3,1},{4,6},{5,7},{6,4},{7,5},{8,10},{9,11},{10,... | collective-permute-start | bytes 1572872 | tf_op jit(solution)/shard_map/ppermute | solution.py:269
  4.7 3.6 %collective-permute-start.4 = (bf16[256,512]{1,0:T(8,128)(2,1)S(1)}, bf16[256,512]{1,0:T(8,128)(2,1)}, u32[]{:S(2)}, u32[]{:S(2)}) collective-permute-start(bf16[256,512]{1,0:T(8,128)(2,1)S(1)} %constant_dynamic-slice_fusion), channel_id=1, source_target_pairs={{0,12},{1,13},{2,14},{3,15},{4,8},{5,9},{6,10},{7,11},{8,4},{9,5},... | collective-permute-start | bytes 786440 | tf_op jit(solution)/shard_map/ppermute | solution.py:269
  8.3 0.0 collective-permute-start.3
  8.3 0.8 copy-done.15
  9.2 0.7 copy-done.18
  9.8 1.6 %shard_map.102 = bf16[16,16,128]{2,1,0:T(8,128)(2,1)} custom-call(s32[16]{0:T(128)S(1)} %bitcast.4, bf16[16,2048]{1,0:T(8,128)(2,1)S(1)} %copy-done.15), custom_call_target="tpu_custom_call" | custom-call | bytes 131072 | tf_op jit(solution)/shard_map/pallas_call | solution.py:26
  11.4 3.5 %all-to-all-start = ((bf16[16,16,128]{2,1,0:T(8,128)(2,1)}), bf16[16,16,128]{2,1,0:T(8,128)(2,1)S(1)}, u32[]{:S(2)}, u32[]{:S(2)}) async-start(bf16[16,16,128]{2,1,0:T(8,128)(2,1)} %shard_map.102), calls=%async_computation | async-start | bytes 131072 | tf_op jit(solution)/shard_map/all_to_all | solution.py:285
  15.0 0.1 pad_add_fusion.meta
  15.0 1.2 %copy-done.7 = bf16[16,64,512]{2,1,0:T(8,128)(2,1)S(1)} copy-done((bf16[16,64,512]{2,1,0:T(8,128)(2,1)S(1)}, bf16[16,64,512]{2,1,0:T(8,128)(2,1)}, u32[]{:S(2)}) %copy-start.7) | copy-done | bytes 1048600
  16.3 0.7 copy-done.19
  16.9 0.0 copy-start
  16.9 0.6 shard_map.104
  17.6 0.0 copy-start.2
  17.6 1.0 copy-done.2
  18.6 2.9 %collective-permute-done.3.refs_2_ = bf16[256,512]{1,0:T(8,128)(2,1)S(1)} collective-permute-done((bf16[256,512]{1,0:T(8,128)(2,1)S(1)}, bf16[256,512]{1,0:T(8,128)(2,1)S(1)}, u32[]{:S(2)}, u32[]{:S(2)}) %collective-permute-start.3) | collective-permute-done | bytes 262176 | tf_op jit(solution)/shard_map/ppermute | solution.py:269
  21.4 0.4 all-to-all-done.packed
  21.8 0.3 copy-done.23
  22.1 0.2 copy-done.22
  22.3 4.9 %all-to-all-start.1 = ((bf16[8,128,512]{2,1,0:T(8,128)(2,1)}), bf16[8,128,512]{2,1,0:T(8,128)(2,1)S(1)}, u32[]{:S(2)}, u32[]{:S(2)}) async-start(bf16[8,128,512]{2,1,0:T(8,128)(2,1)} %copy-done.2), calls=%async_computation.1 | async-start | bytes 2097152 | tf_op jit(solution)/shard_map/all_to_all | solution.py:277
  27.2 2.0 %collective-permute-start.13 = (bf16[256,512]{1,0:T(8,128)(2,1)}, bf16[256,512]{1,0:T(8,128)(2,1)S(1)}, u32[]{:S(2)}, u32[]{:S(2)}) collective-permute-start(bf16[256,512]{1,0:T(8,128)(2,1)} %collective-permute-done.4.refs_6_), channel_id=1, source_target_pairs={{0,4},{1,5},{2,6},{3,7},{4,0},{5,1},{6,2},{7,3},{8,12},{9,13},{10,... | collective-permute-start | bytes 786440 | tf_op jit(solution)/shard_map/ppermute | solution.py:269
  29.2 1.5 %collective-permute-start.11 = (bf16[256,512]{1,0:T(8,128)(2,1)}, bf16[256,512]{1,0:T(8,128)(2,1)S(1)}, u32[]{:S(2)}, u32[]{:S(2)}) collective-permute-start(bf16[256,512]{1,0:T(8,128)(2,1)} %collective-permute-done.4.refs_6_), channel_id=1, source_target_pairs={{0,2},{1,3},{2,0},{3,1},{4,6},{5,7},{6,4},{7,5},{8,10},{9,11},{10,... | collective-permute-start | bytes 786440 | tf_op jit(solution)/shard_map/ppermute | solution.py:269
  30.7 1.1 %shard_map.103 = (bf16[512,64]{1,0:T(8,128)(2,1)S(1)}, bf16[128,64]{1,0:T(8,128)(2,1)S(1)}) custom-call(s32[3]{0:T(128)S(1)} %pad_add_fusion.meta, s32[16]{0:T(128)S(1)} %bitcast.6, s32[16]{0:T(128)S(1)} %copy-done.21, bf16[128,512]{1,0:T(8,128)(2,1)S(1)} %copy-done.6, bf16[16,16,128]{2,1,0:T(8,128)(2,1)S(1)} %all-to-all-done.packed), custom_call_target="tpu_custom_call" | custom-call | bytes 278528 | tf_op jit(solution)/shard_map/pallas_call | solution.py:26
  31.8 0.6 copy-done.13
  32.4 0.0 collective-permute-start.6
  32.4 1.5 %collective-permute-start.10 = (bf16[256,512]{1,0:T(8,128)(2,1)}, bf16[256,512]{1,0:T(8,128)(2,1)S(1)}, u32[]{:S(2)}, u32[]{:S(2)}) collective-permute-start(bf16[256,512]{1,0:T(8,128)(2,1)} %collective-permute-done.4.refs_6_), channel_id=1, source_target_pairs={{0,16},{1,17},{2,18},{3,19},{4,20},{5,21},{6,22},{7,23},{8,24},{9,... | collective-permute-start | bytes 786440 | tf_op jit(solution)/shard_map/ppermute | solution.py:269
  33.9 0.6 collective-permute-start.8
  34.5 0.6 collective-permute-start.7
  35.1 15.7 %collective-permute-done.13.refs_10_ = bf16[256,512]{1,0:T(8,128)(2,1)S(1)} collective-permute-done((bf16[256,512]{1,0:T(8,128)(2,1)}, bf16[256,512]{1,0:T(8,128)(2,1)S(1)}, u32[]{:S(2)}, u32[]{:S(2)}) %collective-permute-start.13) | collective-permute-done | bytes 262176 | tf_op jit(solution)/shard_map/ppermute | solution.py:269
  50.9 1.1 %collective-permute-start.15 = (bf16[256,512]{1,0:T(8,128)(2,1)S(1)}, bf16[256,512]{1,0:T(8,128)(2,1)S(1)}, u32[]{:S(2)}, u32[]{:S(2)}) collective-permute-start(bf16[256,512]{1,0:T(8,128)(2,1)S(1)} %collective-permute-done.13.refs_10_), channel_id=1, source_target_pairs={{0,2},{1,3},{2,0},{3,1},{4,6},{5,7},{6,4},{7,5},{8,10},{9,11},{10,... | collective-permute-start | bytes 786440 | tf_op jit(solution)/shard_map/ppermute | solution.py:269
  52.0 0.0 collective-permute-done.11.refs_8_
  52.0 1.5 %collective-permute-start.12 = (bf16[256,512]{1,0:T(8,128)(2,1)S(1)}, bf16[256,512]{1,0:T(8,128)(2,1)}, u32[]{:S(2)}, u32[]{:S(2)}) collective-permute-start(bf16[256,512]{1,0:T(8,128)(2,1)S(1)} %collective-permute-done.11.refs_8_), channel_id=1, source_target_pairs={{0,16},{1,17},{2,18},{3,19},{4,20},{5,21},{6,22},{7,23},{8,24},{9,... | collective-permute-start | bytes 786440 | tf_op jit(solution)/shard_map/ppermute | solution.py:269
  53.5 2.1 %shard_map.106 = (bf16[8,64,512]{2,1,0:T(8,128)(2,1)S(1)}, bf16[8,80,512]{2,1,0:T(8,128)(2,1)S(1)}) custom-call(s32[3]{0:T(128)S(1)} %pad_add_fusion.meta, bf16[128,8192]{1,0:T(8,128)(2,1)S(1)} %copy-done, bf16[128,8192]{1,0:T(8,128)(2,1)} %collective-permute-done.tok_sib, bf16[128,64]{1,0:T(8,128)(2,1)S(1)} %get-tuple-element.30.back_own, ...), custom_call_target="tpu_custom_call" | custom-call | flops 134217728 | bytes 5406720 | tf_op jit(solution)/shard_map/pallas_call | solution.py:26
  55.6 0.0 copy-start.3
  55.6 0.8 copy-done.3
  56.4 0.8 copy-done.9
  57.2 0.0 collective-permute-done.10.refs_7_
  57.2 0.0 collective-permute-done.8.refs_4_
  57.3 1.1 %collective-permute-done.15.refs_12_ = bf16[256,512]{1,0:T(8,128)(2,1)S(1)} collective-permute-done((bf16[256,512]{1,0:T(8,128)(2,1)S(1)}, bf16[256,512]{1,0:T(8,128)(2,1)S(1)}, u32[]{:S(2)}, u32[]{:S(2)}) %collective-permute-start.15) | collective-permute-done | bytes 262176 | tf_op jit(solution)/shard_map/ppermute | solution.py:269
  58.4 0.7 copy-done.29
  59.1 0.0 all-to-all-done.1.blocks
  59.1 5.8 %all-to-all-start.2 = ((bf16[8,64,512]{2,1,0:T(8,128)(2,1)}), bf16[8,64,512]{2,1,0:T(8,128)(2,1)}, u32[]{:S(2)}, u32[]{:S(2)}) async-start(bf16[8,64,512]{2,1,0:T(8,128)(2,1)} %copy-done.9), calls=%async_computation.2 | async-start | bytes 1048576 | tf_op jit(solution)/shard_map/all_to_all | solution.py:277
  64.9 1.6 %collective-permute-start.14 = (bf16[256,512]{1,0:T(8,128)(2,1)}, bf16[256,512]{1,0:T(8,128)(2,1)}, u32[]{:S(2)}, u32[]{:S(2)}) collective-permute-start(bf16[256,512]{1,0:T(8,128)(2,1)} %copy-done.24), channel_id=1, source_target_pairs={{0,16},{1,17},{2,18},{3,19},{4,20},{5,21},{6,22},{7,23},{8,24},{9,... | collective-permute-start | bytes 786440 | tf_op jit(solution)/shard_map/ppermute | solution.py:269
  66.4 0.5 collective-permute-start.9
  67.0 1.5 %collective-permute-start.16 = (bf16[256,512]{1,0:T(8,128)(2,1)}, bf16[256,512]{1,0:T(8,128)(2,1)}, u32[]{:S(2)}, u32[]{:S(2)}) collective-permute-start(bf16[256,512]{1,0:T(8,128)(2,1)} %copy-done.29), channel_id=1, source_target_pairs={{0,16},{1,17},{2,18},{3,19},{4,20},{5,21},{6,22},{7,23},{8,24},{9,... | collective-permute-start | bytes 786440 | tf_op jit(solution)/shard_map/ppermute | solution.py:269
  68.5 2.3 %shard_map.105.low = f32[256,64]{1,0:T(8,128)S(1)} custom-call(s32[3]{0:T(128)S(1)} %pad_add_fusion.meta, bf16[128,8192]{1,0:T(8,128)(2,1)S(1)} %copy-done, bf16[128,8192]{1,0:T(8,128)(2,1)} %collective-permute-done.tok_sib, bf16[8,128,512]{2,1,0:T(8,128)(2,1)S(1)} %all-to-all-done.1.blocks), custom_call_target="tpu_custom_call" | custom-call | flops 134217728 | bytes 5308416 | tf_op jit(solution)/shard_map/pallas_call | solution.py:26
  70.8 0.1 collective-permute-start.5
  70.8 1.3 %collective-permute-done.5.other = f32[256,64]{1,0:T(8,128)S(1)} collective-permute-done((f32[256,64]{1,0:T(8,128)S(1)}, f32[256,64]{1,0:T(8,128)S(1)}, u32[]{:S(2)}, u32[]{:S(2)}) %collective-permute-start.5) | collective-permute-done | bytes 65568 | tf_op jit(solution)/shard_map/ppermute | solution.py:269
  72.2 1.6 %shard_map.107 = (f32[128,512]{1,0:T(8,128)S(1)}, bf16[8,80,512]{2,1,0:T(8,128)(2,1)S(1)}) custom-call(s32[3]{0:T(128)S(1)} %pad_add_fusion.meta, s32[16]{0:T(128)S(1)} %bitcast.7, s32[16]{0:T(128)S(1)} %copy-done.21, f32[256,64]{1,0:T(8,128)S(1)} %shard_map.105.low, f32[256,64]{1,0:T(8,128)S(1)} %collective-permute-done.5.other, ...), custom_call_target="tpu_custom_call", output_to_operand_aliasing={{1}: (8, {})} | custom-call | tf_op jit(solution)/shard_map/pallas_call | solution.py:315
  73.8 0.8 copy-done.5
  74.6 3.3 %all-to-all-done.2.first = bf16[8,64,512]{2,1,0:T(8,128)(2,1)} async-done(((bf16[8,64,512]{2,1,0:T(8,128)(2,1)}), bf16[8,64,512]{2,1,0:T(8,128)(2,1)}, u32[]{:S(2)}, u32[]{:S(2)}) %all-to-all-start.2) | async-done | bytes 524320 | tf_op jit(solution)/shard_map/all_to_all | solution.py:277
  78.0 3.5 %all-to-all-start.3 = ((bf16[8,80,512]{2,1,0:T(8,128)(2,1)}), bf16[8,80,512]{2,1,0:T(8,128)(2,1)S(1)}, u32[]{:S(2)}, u32[]{:S(2)}) async-start(bf16[8,80,512]{2,1,0:T(8,128)(2,1)} %copy-done.5), calls=%async_computation.3 | async-start | bytes 1310720 | tf_op jit(solution)/shard_map/all_to_all | solution.py:277
  81.5 0.0 collective-permute-done.14.refs_11_
  81.5 0.0 collective-permute-done.9.refs_5_
  81.5 1.1 %collective-permute-done.16.refs_13_ = bf16[256,512]{1,0:T(8,128)(2,1)} collective-permute-done((bf16[256,512]{1,0:T(8,128)(2,1)}, bf16[256,512]{1,0:T(8,128)(2,1)}, u32[]{:S(2)}, u32[]{:S(2)}) %collective-permute-start.16) | collective-permute-done | bytes 262176 | tf_op jit(solution)/shard_map/ppermute | solution.py:269
  82.6 8.4 %shard_map.108 = (f32[128,512]{1,0:T(8,128)}, f32[128,512]{1,0:T(8,128)}, bf16[128,8192]{1,0:T(8,128)(2,1)}, bf16[128,4096]{1,0:T(8,128)(2,1)}) custom-call(s32[3]{0:T(128)} %copy-done.16, bf16[128,8192]{1,0:T(8,128)(2,1)} %tok_own.5, bf16[128,8192]{1,0:T(8,128)(2,1)} %collective-permute-done.tok_sib, bf16[128,512]{1,0:T(8,128)(2,1)} %og_own.3, ...), custom_call_target="tpu_custom_call" | custom-call | flops 2147483648 | bytes 13402112 | tf_op jit(solution)/shard_map/pallas_call | solution.py:26
  91.1 0.5 collective-permute-start.17
  91.6 2.7 %collective-permute-done.17.other = f32[128,512]{1,0:T(8,128)S(1)} collective-permute-done((f32[128,512]{1,0:T(8,128)}, f32[128,512]{1,0:T(8,128)S(1)}, u32[]{:S(2)}, u32[]{:S(2)}) %collective-permute-start.17) | collective-permute-done | bytes 262176 | tf_op jit(solution)/shard_map/ppermute | solution.py:269
  94.3 0.0 collective-permute-done.18.grad_other
  94.3 0.9 copy-done.10
  95.3 2.2 %shard_map.109 = (bf16[128,512]{1,0:T(8,128)(2,1)}, bf16[128,8192]{1,0:T(8,128)(2,1)}) custom-call(s32[3]{0:T(128)S(1)} %copy-done.17, f32[128,512]{1,0:T(8,128)S(1)} %copy-done.10, f32[128,512]{1,0:T(8,128)S(1)} %collective-permute-done.17.other, f32[128,512]{1,0:T(8,128)S(1)} %get-tuple-element.29.out_low, ...), custom_call_target="tpu_custom_call", output_to_operand_aliasing={{1}: (5, {})} | custom-call | tf_op jit(solution)/shard_map/pallas_call | solution.py:336
  97.5 0.7 all-to-all-done.3.second
  98.2 2.1 %shard_map.110 = (bf16[16,64,512]{2,1,0:T(8,128)(2,1)}, bf16[16,2048]{1,0:T(8,128)(2,1)}) custom-call(s32[3]{0:T(128)S(1)} %copy-done.17, s32[16]{0:T(128)S(1)} %bitcast.8, bf16[8,64,512]{2,1,0:T(8,128)(2,1)} %all-to-all-done.2.first, bf16[8,80,512]{2,1,0:T(8,128)(2,1)S(1)} %all-to-all-done.3.second), custom_call_target="tpu_custom_call" | custom-call | bytes 2293760 | tf_op jit(solution)/shard_map/pallas_call | solution.py:26
  (53 shorter events, 0.1 us)
Async XLA Ops:
  0.6 20.8 %collective-permute-start = (bf16[128,8192]{1,0:T(8,128)(2,1)}, bf16[128,8192]{1,0:T(8,128)(2,1)}, u32[]{:S(2)}, u32[]{:S(2)}) collective-permute-start(bf16[128,8192]{1,0:T(8,128)(2,1)} %tok_own.5), channel_id=1, source_target_pairs={{0,1},{1,0},{2,3},{3,2},{4,5},{5,4},{6,7},{7,6},{8,9},{9,8},{10,11... | collective-permute-start | bytes 6291464 | tf_op jit(solution)/shard_map/ppermute | solution.py:269
  2.1 19.3 %collective-permute-start.2 = (bf16[512,512]{1,0:T(8,128)(2,1)}, bf16[512,512]{1,0:T(8,128)(2,1)S(1)}, u32[]{:S(2)}, u32[]{:S(2)}) collective-permute-start(bf16[512,512]{1,0:T(8,128)(2,1)} %refs_0_.1), channel_id=1, source_target_pairs={{0,2},{1,3},{2,0},{3,1},{4,6},{5,7},{6,4},{7,5},{8,10},{9,11},{10,... | collective-permute-start | bytes 1572872 | tf_op jit(solution)/shard_map/ppermute | solution.py:269
  4.7 13.8 %collective-permute-start.4 = (bf16[256,512]{1,0:T(8,128)(2,1)S(1)}, bf16[256,512]{1,0:T(8,128)(2,1)}, u32[]{:S(2)}, u32[]{:S(2)}) collective-permute-start(bf16[256,512]{1,0:T(8,128)(2,1)S(1)} %constant_dynamic-slice_fusion), channel_id=1, source_target_pairs={{0,12},{1,13},{2,14},{3,15},{4,8},{5,9},{6,10},{7,11},{8,4},{9,5},... | collective-permute-start | bytes 786440 | tf_op jit(solution)/shard_map/ppermute | solution.py:269
  8.3 13.1 %collective-permute-start.3 = (bf16[256,512]{1,0:T(8,128)(2,1)S(1)}, bf16[256,512]{1,0:T(8,128)(2,1)S(1)}, u32[]{:S(2)}, u32[]{:S(2)}) collective-permute-start(bf16[256,512]{1,0:T(8,128)(2,1)S(1)} %constant_dynamic-slice_fusion), channel_id=1, source_target_pairs={{0,4},{1,5},{2,6},{3,7},{4,0},{5,1},{6,2},{7,3},{8,12},{9,13},{10,... | collective-permute-start | bytes 786440 | tf_op jit(solution)/shard_map/ppermute | solution.py:269
  8.3 10.2 %collective-permute-start.1 = (bf16[128,512]{1,0:T(8,128)(2,1)}, bf16[128,512]{1,0:T(8,128)(2,1)S(1)}, u32[]{:S(2)}, u32[]{:S(2)}) collective-permute-start(bf16[128,512]{1,0:T(8,128)(2,1)} %og_own.3), channel_id=1, source_target_pairs={{0,1},{1,0},{2,3},{3,2},{4,5},{5,4},{6,7},{7,6},{8,9},{9,8},{10,11... | collective-permute-start | bytes 393224 | tf_op jit(solution)/shard_map/ppermute | solution.py:269
  8.3 0.8 copy-start.15
  9.2 0.7 copy-start.18
  11.4 10.4 %all-to-all-start = ((bf16[16,16,128]{2,1,0:T(8,128)(2,1)}), bf16[16,16,128]{2,1,0:T(8,128)(2,1)S(1)}, u32[]{:S(2)}, u32[]{:S(2)}) async-start(bf16[16,16,128]{2,1,0:T(8,128)(2,1)} %shard_map.102), calls=%async_computation | async-start | bytes 131072 | tf_op jit(solution)/shard_map/all_to_all | solution.py:285
  15.0 1.2 %copy-start.7 = (bf16[16,64,512]{2,1,0:T(8,128)(2,1)S(1)}, bf16[16,64,512]{2,1,0:T(8,128)(2,1)}, u32[]{:S(2)}) copy-start(bf16[16,64,512]{2,1,0:T(8,128)(2,1)} %down.1) | copy-start | bytes 3145732
  16.3 0.7 copy-start.19
  16.9 55.3 %copy-start.16 = (s32[3]{0:T(128)}, s32[3]{0:T(128)S(1)}, u32[]{:S(2)}) copy-start(s32[3]{0:T(128)S(1)} %pad_add_fusion.meta) | copy-start | bytes 40
  16.9 13.7 %copy-start.6 = (bf16[128,512]{1,0:T(8,128)(2,1)S(1)}, bf16[128,512]{1,0:T(8,128)(2,1)}, u32[]{:S(2)}) copy-start(bf16[128,512]{1,0:T(8,128)(2,1)} %og_own.3) | copy-start | bytes 393220
  16.9 13.7 %copy-start.20 = (s32[16,1]{0,1:T(1,128)S(1)}, s32[16,1]{0,1:T(1,128)}, u32[]{:S(2)}) copy-start(s32[16,1]{0,1:T(1,128)} %param.13) | copy-start | bytes 196
  16.9 13.7 %copy-start.21 = (s32[16]{0:T(128)S(1)}, s32[16]{0:T(128)}, u32[]{:S(2)}) copy-start(s32[16]{0:T(128)} %ranks.3) | copy-start | bytes 196
  16.9 36.5 %copy-start = (bf16[128,8192]{1,0:T(8,128)(2,1)S(1)}, bf16[128,8192]{1,0:T(8,128)(2,1)}, u32[]{:S(2)}) copy-start(bf16[128,8192]{1,0:T(8,128)(2,1)} %tok_own.5) | copy-start | bytes 6291460
  17.6 1.0 copy-start.2
  18.5 53.6 %copy-start.8 = (bf16[128,512]{1,0:T(8,128)(2,1)}, bf16[128,512]{1,0:T(8,128)(2,1)S(1)}, u32[]{:S(2)}) copy-start(bf16[128,512]{1,0:T(8,128)(2,1)S(1)} %collective-permute-done.1.og_sib) | copy-start | bytes 393220
  21.4 0.7 copy-start.23
  21.4 0.9 copy-start.22
  22.3 36.8 %all-to-all-start.1 = ((bf16[8,128,512]{2,1,0:T(8,128)(2,1)}), bf16[8,128,512]{2,1,0:T(8,128)(2,1)S(1)}, u32[]{:S(2)}, u32[]{:S(2)}) async-start(bf16[8,128,512]{2,1,0:T(8,128)(2,1)} %copy-done.2), calls=%async_computation.1 | async-start | bytes 2097152 | tf_op jit(solution)/shard_map/all_to_all | solution.py:277
  27.2 23.7 %collective-permute-start.13 = (bf16[256,512]{1,0:T(8,128)(2,1)}, bf16[256,512]{1,0:T(8,128)(2,1)S(1)}, u32[]{:S(2)}, u32[]{:S(2)}) collective-permute-start(bf16[256,512]{1,0:T(8,128)(2,1)} %collective-permute-done.4.refs_6_), channel_id=1, source_target_pairs={{0,4},{1,5},{2,6},{3,7},{4,0},{5,1},{6,2},{7,3},{8,12},{9,13},{10,... | collective-permute-start | bytes 786440 | tf_op jit(solution)/shard_map/ppermute | solution.py:269
  29.2 22.8 %collective-permute-start.11 = (bf16[256,512]{1,0:T(8,128)(2,1)}, bf16[256,512]{1,0:T(8,128)(2,1)S(1)}, u32[]{:S(2)}, u32[]{:S(2)}) collective-permute-start(bf16[256,512]{1,0:T(8,128)(2,1)} %collective-permute-done.4.refs_6_), channel_id=1, source_target_pairs={{0,2},{1,3},{2,0},{3,1},{4,6},{5,7},{6,4},{7,5},{8,10},{9,11},{10,... | collective-permute-start | bytes 786440 | tf_op jit(solution)/shard_map/ppermute | solution.py:269
  31.8 0.6 copy-start.13
  32.4 23.1 %copy-start.11 = (bf16[128,64]{1,0:T(8,128)(2,1)}, bf16[128,64]{1,0:T(8,128)(2,1)S(1)}, u32[]{:S(2)}) copy-start(bf16[128,64]{1,0:T(8,128)(2,1)S(1)} %get-tuple-element.30.back_own) | copy-start | bytes 49156
  32.4 2.1 %collective-permute-start.6 = (bf16[128,64]{1,0:T(8,128)(2,1)S(1)}, bf16[128,64]{1,0:T(8,128)(2,1)S(1)}, u32[]{:S(2)}, u32[]{:S(2)}) collective-permute-start(bf16[128,64]{1,0:T(8,128)(2,1)S(1)} %get-tuple-element.30.back_own), channel_id=1, source_target_pairs={{0,1},{1,0},{2,3},{3,2},{4,5},{5,4},{6,7},{7,6},{8,9},{9,8},{10,11... | collective-permute-start | bytes 49160 | tf_op jit(solution)/shard_map/ppermute | solution.py:269
  32.4 24.8 %collective-permute-start.10 = (bf16[256,512]{1,0:T(8,128)(2,1)}, bf16[256,512]{1,0:T(8,128)(2,1)S(1)}, u32[]{:S(2)}, u32[]{:S(2)}) collective-permute-start(bf16[256,512]{1,0:T(8,128)(2,1)} %collective-permute-done.4.refs_6_), channel_id=1, source_target_pairs={{0,16},{1,17},{2,18},{3,19},{4,20},{5,21},{6,22},{7,23},{8,24},{9,... | collective-permute-start | bytes 786440 | tf_op jit(solution)/shard_map/ppermute | solution.py:269
  33.9 23.3 %collective-permute-start.8 = (bf16[256,512]{1,0:T(8,128)(2,1)}, bf16[256,512]{1,0:T(8,128)(2,1)S(1)}, u32[]{:S(2)}, u32[]{:S(2)}) collective-permute-start(bf16[256,512]{1,0:T(8,128)(2,1)} %copy-done.23), channel_id=1, source_target_pairs={{0,2},{1,3},{2,0},{3,1},{4,6},{5,7},{6,4},{7,5},{8,10},{9,11},{10,... | collective-permute-start | bytes 786440 | tf_op jit(solution)/shard_map/ppermute | solution.py:269
  34.5 21.1 %copy-start.12 = (bf16[128,64]{1,0:T(8,128)(2,1)}, bf16[128,64]{1,0:T(8,128)(2,1)S(1)}, u32[]{:S(2)}) copy-start(bf16[128,64]{1,0:T(8,128)(2,1)S(1)} %collective-permute-done.6.back_sib) | copy-start | bytes 49156
  34.5 22.8 %collective-permute-start.7 = (bf16[256,512]{1,0:T(8,128)(2,1)}, bf16[256,512]{1,0:T(8,128)(2,1)S(1)}, u32[]{:S(2)}, u32[]{:S(2)}) collective-permute-start(bf16[256,512]{1,0:T(8,128)(2,1)} %copy-done.23), channel_id=1, source_target_pairs={{0,16},{1,17},{2,18},{3,19},{4,20},{5,21},{6,22},{7,23},{8,24},{9,... | collective-permute-start | bytes 786440 | tf_op jit(solution)/shard_map/ppermute | solution.py:269
  50.9 4.7 %copy-start.24 = (bf16[256,512]{1,0:T(8,128)(2,1)}, bf16[256,512]{1,0:T(8,128)(2,1)S(1)}, u32[]{:S(2)}) copy-start(bf16[256,512]{1,0:T(8,128)(2,1)S(1)} %collective-permute-done.13.refs_10_) | copy-start | bytes 786436
  50.9 7.5 %collective-permute-start.15 = (bf16[256,512]{1,0:T(8,128)(2,1)S(1)}, bf16[256,512]{1,0:T(8,128)(2,1)S(1)}, u32[]{:S(2)}, u32[]{:S(2)}) collective-permute-start(bf16[256,512]{1,0:T(8,128)(2,1)S(1)} %collective-permute-done.13.refs_10_), channel_id=1, source_target_pairs={{0,2},{1,3},{2,0},{3,1},{4,6},{5,7},{6,4},{7,5},{8,10},{9,11},{10,... | collective-permute-start | bytes 786440 | tf_op jit(solution)/shard_map/ppermute | solution.py:269
  52.0 3.6 %copy-start.25 = (bf16[256,512]{1,0:T(8,128)(2,1)}, bf16[256,512]{1,0:T(8,128)(2,1)S(1)}, u32[]{:S(2)}) copy-start(bf16[256,512]{1,0:T(8,128)(2,1)S(1)} %collective-permute-done.11.refs_8_) | copy-start | bytes 786436
  52.0 7.1 %collective-permute-start.12 = (bf16[256,512]{1,0:T(8,128)(2,1)S(1)}, bf16[256,512]{1,0:T(8,128)(2,1)}, u32[]{:S(2)}, u32[]{:S(2)}) collective-permute-start(bf16[256,512]{1,0:T(8,128)(2,1)S(1)} %collective-permute-done.11.refs_8_), channel_id=1, source_target_pairs={{0,16},{1,17},{2,18},{3,19},{4,20},{5,21},{6,22},{7,23},{8,24},{9,... | collective-permute-start | bytes 786440 | tf_op jit(solution)/shard_map/ppermute | solution.py:269
  55.6 0.8 copy-start.3
  56.4 0.8 copy-start.9
  57.2 1.1 %copy-start.26 = (bf16[256,512]{1,0:T(8,128)(2,1)}, bf16[256,512]{1,0:T(8,128)(2,1)S(1)}, u32[]{:S(2)}) copy-start(bf16[256,512]{1,0:T(8,128)(2,1)S(1)} %collective-permute-done.10.refs_7_) | copy-start | bytes 786436
  57.2 1.1 %copy-start.27 = (bf16[256,512]{1,0:T(8,128)(2,1)}, bf16[256,512]{1,0:T(8,128)(2,1)S(1)}, u32[]{:S(2)}) copy-start(bf16[256,512]{1,0:T(8,128)(2,1)S(1)} %collective-permute-done.8.refs_4_) | copy-start | bytes 786436
  57.2 1.1 %copy-start.28 = (bf16[256,512]{1,0:T(8,128)(2,1)}, bf16[256,512]{1,0:T(8,128)(2,1)S(1)}, u32[]{:S(2)}) copy-start(bf16[256,512]{1,0:T(8,128)(2,1)S(1)} %collective-permute-done.7.refs_3_) | copy-start | bytes 786436
  58.4 0.7 copy-start.29
  59.1 11.7 %copy-start.1 = (bf16[8,128,512]{2,1,0:T(8,128)(2,1)}, bf16[8,128,512]{2,1,0:T(8,128)(2,1)S(1)}, u32[]{:S(2)}) copy-start(bf16[8,128,512]{2,1,0:T(8,128)(2,1)S(1)} %all-to-all-done.1.blocks) | copy-start | bytes 3145732
  59.1 18.9 %all-to-all-start.2 = ((bf16[8,64,512]{2,1,0:T(8,128)(2,1)}), bf16[8,64,512]{2,1,0:T(8,128)(2,1)}, u32[]{:S(2)}, u32[]{:S(2)}) async-start(bf16[8,64,512]{2,1,0:T(8,128)(2,1)} %copy-done.9), calls=%async_computation.2 | async-start | bytes 1048576 | tf_op jit(solution)/shard_map/all_to_all | solution.py:277
  64.9 7.3 %copy-start.4 = (bf16[8,80,512]{2,1,0:T(8,128)(2,1)S(1)}, bf16[8,80,512]{2,1,0:T(8,128)(2,1)}, u32[]{:S(2)}) copy-start(bf16[8,80,512]{2,1,0:T(8,128)(2,1)} %copy-done.3) | copy-start | bytes 1966084
  64.9 7.3 %copy-start.14 = (bf16[512,64]{1,0:T(8,128)(2,1)S(1)}, bf16[512,64]{1,0:T(8,128)(2,1)}, u32[]{:S(2)}) copy-start(bf16[512,64]{1,0:T(8,128)(2,1)} %copy-done.13) | copy-start | bytes 196612
  64.9 16.6 %collective-permute-start.14 = (bf16[256,512]{1,0:T(8,128)(2,1)}, bf16[256,512]{1,0:T(8,128)(2,1)}, u32[]{:S(2)}, u32[]{:S(2)}) collective-permute-start(bf16[256,512]{1,0:T(8,128)(2,1)} %copy-done.24), channel_id=1, source_target_pairs={{0,16},{1,17},{2,18},{3,19},{4,20},{5,21},{6,22},{7,23},{8,24},{9,... | collective-permute-start | bytes 786440 | tf_op jit(solution)/shard_map/ppermute | solution.py:269
  66.4 15.1 %collective-permute-start.9 = (bf16[256,512]{1,0:T(8,128)(2,1)}, bf16[256,512]{1,0:T(8,128)(2,1)}, u32[]{:S(2)}, u32[]{:S(2)}) collective-permute-start(bf16[256,512]{1,0:T(8,128)(2,1)} %copy-done.27), channel_id=1, source_target_pairs={{0,16},{1,17},{2,18},{3,19},{4,20},{5,21},{6,22},{7,23},{8,24},{9,... | collective-permute-start | bytes 786440 | tf_op jit(solution)/shard_map/ppermute | solution.py:269
  67.0 15.6 %collective-permute-start.16 = (bf16[256,512]{1,0:T(8,128)(2,1)}, bf16[256,512]{1,0:T(8,128)(2,1)}, u32[]{:S(2)}, u32[]{:S(2)}) collective-permute-start(bf16[256,512]{1,0:T(8,128)(2,1)} %copy-done.29), channel_id=1, source_target_pairs={{0,16},{1,17},{2,18},{3,19},{4,20},{5,21},{6,22},{7,23},{8,24},{9,... | collective-permute-start | bytes 786440 | tf_op jit(solution)/shard_map/ppermute | solution.py:269
  70.8 1.4 %collective-permute-start.5 = (f32[256,64]{1,0:T(8,128)S(1)}, f32[256,64]{1,0:T(8,128)S(1)}, u32[]{:S(2)}, u32[]{:S(2)}) collective-permute-start(f32[256,64]{1,0:T(8,128)S(1)} %shard_map.105.low), channel_id=1, source_target_pairs={{0,1},{1,0},{2,3},{3,2},{4,5},{5,4},{6,7},{7,6},{8,9},{9,8},{10,11... | collective-permute-start | bytes 196616 | tf_op jit(solution)/shard_map/ppermute | solution.py:269
  73.8 0.8 copy-start.5
  78.0 20.3 %all-to-all-start.3 = ((bf16[8,80,512]{2,1,0:T(8,128)(2,1)}), bf16[8,80,512]{2,1,0:T(8,128)(2,1)S(1)}, u32[]{:S(2)}, u32[]{:S(2)}) async-start(bf16[8,80,512]{2,1,0:T(8,128)(2,1)} %copy-done.5), calls=%async_computation.3 | async-start | bytes 1310720 | tf_op jit(solution)/shard_map/all_to_all | solution.py:277
  81.5 12.8 %copy-start.17 = (s32[3]{0:T(128)S(1)}, s32[3]{0:T(128)}, u32[]{:S(2)}) copy-start(s32[3]{0:T(128)} %copy-done.16) | copy-start | bytes 40
  91.1 3.2 %collective-permute-start.18 = (bf16[128,4096]{1,0:T(8,128)(2,1)}, bf16[128,4096]{1,0:T(8,128)(2,1)S(1)}, u32[]{:S(2)}, u32[]{:S(2)}) collective-permute-start(bf16[128,4096]{1,0:T(8,128)(2,1)} %get-tuple-element.34), channel_id=1, source_target_pairs={{0,1},{1,0},{2,3},{3,2},{4,5},{5,4},{6,7},{7,6},{8,9},{9,8},{10,11... | collective-permute-start | bytes 3145736 | tf_op jit(solution)/shard_map/ppermute | solution.py:269
  91.1 3.2 %collective-permute-start.17 = (f32[128,512]{1,0:T(8,128)}, f32[128,512]{1,0:T(8,128)S(1)}, u32[]{:S(2)}, u32[]{:S(2)}) collective-permute-start(f32[128,512]{1,0:T(8,128)} %get-tuple-element.33), channel_id=1, source_target_pairs={{0,1},{1,0},{2,3},{3,2},{4,5},{5,4},{6,7},{7,6},{8,9},{9,8},{10,11... | collective-permute-start | bytes 786440 | tf_op jit(solution)/shard_map/ppermute | solution.py:269
  94.3 1.0 copy-start.10
